TPU v7x, 256 devices: a whole 4x4x8 slice. The times are simulated.
256 devices in a mesh: zslab: 4 (over x_hi, core), angle: 64 (over y, z, x_lo).
Axes of the slice: x: 4 (x_hi: 2, x_lo: 2; x = x_hi * 2 + x_lo), y: 4, z: 8, core: 2. Of those that a mesh axis runs over, the one named last changes fastest.
Arguments:
- measured: float32 [512, 4, 2048], P('angle', 'zslab'), may hold values from -6 to 6
- basis_time: float32 [32, 8], replicated, may hold values from -2.5 to 2.5
- frame_index: int32 [512], P('angle'), may hold values from 0 to 31
- angle_slot: int32 [512], P('angle'), may hold values from 0 to 3
- proj_weights: bfloat16 [256, 128, 256], P('angle'), may hold values from -0.046875 to 0.046875
- tile_offsets: int32 [256, 64, 16], P('angle'), may hold values from 0 to 14
- cone_weights: float32 [3, 512, 4], P(None, 'angle'), may hold values from 0.3 to 1
Outputs:
- coefficients: bfloat16 [64, 8, 4, 2048], P('angle', None, 'zslab')
- misfit: float32 [512, 4, 2048], P('angle', 'zslab')
All inputs are finite; a program needn't handle non-finite values.
Results may differ from a plain program's by a relative error of at most 0.0065.
Values may be sent and summed in bfloat16 or wider, within the bound.
A program may use at most 64 MiB of HBM per device.

v0:
```python
import jax
import jax.numpy as jnp
from jax import lax
from jax.sharding import PartitionSpec as P

ROWS_DEV = 1


step_scale = 0.4
highest = lax.Precision.HIGHEST


def padded_2(block, sides, width):
    for axis, dim in sides:
        count = lax.axis_size(axis)
        forward = [(i, i + 1) for i in range(count - 1)]
        backward = [(target, source) for source, target in forward]
        low = lax.ppermute(
            lax.slice_in_dim(block, block.shape[dim] - width, None, axis=dim), axis, forward
        )
        high = lax.ppermute(lax.slice_in_dim(block, 0, width, axis=dim), axis, backward)
        block = jnp.concatenate([low, block, high], axis=dim)
    return block


def landing_table(offset_rows, det_tiles):
    pair_steps = jnp.arange(2, dtype=jnp.int32)[:, None]
    targets = offset_rows[:, :, :, None, None] + pair_steps
    return (targets == jnp.arange(det_tiles, dtype=jnp.int32)).astype(jnp.bfloat16)


def block_rows():
    for candidate in (16, 8, 4, 2, 1):
        return candidate
    return 1


def land_parts(landing, response):
    upper = response.astype(jnp.bfloat16)
    lower = (response - upper.astype(jnp.float32)).astype(jnp.bfloat16)
    total = jnp.einsum("ayihj,yiakzhc->akzjc", landing, upper, preferred_element_type=jnp.float32)
    return total + jnp.einsum(
        "ayihj,yiakzhc->akzjc", landing, lower, preferred_element_type=jnp.float32
    )


def local(measured, basis_time, frame_index, angle_slot, proj_weights, tile_offsets, cone_weights):
    angles_here, tile_size, window = proj_weights.shape
    projs_here, slices, det_cols = measured.shape
    det_tiles = det_cols // tile_size
    frames, basis_count = basis_time.shape
    image_width = tile_offsets.shape[2] * tile_size
    frame_picks = (frame_index[:, None] == jnp.arange(frames, dtype=jnp.int32)).astype(jnp.float32)
    phi_rows = jnp.dot(
        frame_picks, basis_time, precision=highest, preferred_element_type=jnp.float32
    )
    owner_mask = (angle_slot[:, None] == jnp.arange(angles_here, dtype=jnp.int32)).astype(
        jnp.float32
    )
    select = (owner_mask[:, :, None] * phi_rows[:, None, :]).reshape(
        projs_here, angles_here * basis_count
    )
    zstart = lax.axis_index("zslab") * slices
    weight_view = proj_weights.reshape(angles_here, tile_size, 2, tile_size)
    cone_here = lax.dynamic_slice_in_dim(cone_weights, zstart, slices, 2)
    cone_pad = jnp.pad(cone_weights, ((0, 0), (0, 0), (1, 1)))
    cone_window = lax.dynamic_slice_in_dim(cone_pad, zstart, slices + 2, 2)

    def project_block(running, rows_coef, offset_rows):
        block = rows_coef.shape[0]
        pixel_tiles = rows_coef.reshape(
            block, basis_count, slices, image_width // tile_size, tile_size
        )
        response = jnp.einsum(
            "ykziu,aud->yiakzd", pixel_tiles, proj_weights, preferred_element_type=jnp.float32
        )
        response = response.reshape(
            block, image_width // tile_size, angles_here, basis_count, slices, 2, tile_size
        )
        landing = landing_table(offset_rows, det_tiles)
        return running + land_parts(landing, response)

    def make_term(residual):
        padded = padded_2(residual, (("zslab", 1),), 1)
        back_planes = (
            cone_window[0][:, 2:, None] * padded[:, 2:]
            + cone_window[1][:, 1:-1, None] * padded[:, 1:-1]
            + cone_window[2][:, :-2, None] * padded[:, :-2]
        )
        spread = lax.dot_general(
            select,
            back_planes.reshape(projs_here, slices * det_cols),
            (((0,), (0,)), ((), ())),
            precision=highest,
            preferred_element_type=jnp.float32,
        )
        spread = spread.astype(jnp.bfloat16).reshape(
            angles_here, basis_count, slices, det_tiles, tile_size
        )

        def term(first_row, row_count):
            block = block_rows()

            def term_one_block(step_index, running):
                block_start = step_index * block
                offset_rows = lax.dynamic_slice_in_dim(tile_offsets, block_start, block, 1)
                landing = landing_table(offset_rows, det_tiles)
                picked = jnp.einsum(
                    "ayihj,akzjc->yiakzhc", landing, spread, preferred_element_type=jnp.float32
                ).astype(jnp.bfloat16)
                rows_grad = jnp.einsum(
                    "yiakzhc,auhc->ykziu", picked, weight_view, preferred_element_type=jnp.float32
                )
                rows_grad = rows_grad.reshape(block, basis_count, slices, image_width)
                return lax.dynamic_update_slice_in_dim(running, rows_grad, block_start, 0)

            blank_rows = jnp.zeros((row_count, basis_count, slices, image_width), jnp.float32)
            return lax.fori_loop(0, row_count // block, term_one_block, blank_rows)

        return term

    def scatter_rows(term):
        return lax.psum_scatter(
            term(jnp.int32(0), ROWS_DEV * lax.axis_size("angle")),
            "angle",
            scatter_dimension=0,
            tiled=True,
        )

    first_term = make_term(measured)
    planes_zero = jnp.zeros((angles_here, basis_count, slices, det_tiles, tile_size), jnp.float32)
    first_own = (step_scale * scatter_rows(first_term)).astype(jnp.bfloat16)
    row_piece = lax.all_gather(first_own, "angle", axis=0, tiled=True)
    row_count = row_piece.shape[0]
    block = block_rows()

    def fold_one_block(step_index, carried):
        block_start = step_index * block
        rows_coef = lax.dynamic_slice_in_dim(row_piece, block_start, block, 0)
        offset_rows = lax.dynamic_slice_in_dim(tile_offsets, block_start, block, 1)
        return project_block(carried, rows_coef, offset_rows)

    planes_sum = lax.fori_loop(0, row_count // block, fold_one_block, planes_zero)
    flat_planes = planes_sum.reshape(angles_here * basis_count, slices * det_cols)
    planes_now = jnp.dot(select, flat_planes, precision=highest, preferred_element_type=jnp.float32)
    planes_now = planes_now.reshape(projs_here, slices, det_cols)
    padded = padded_2(planes_now.astype(jnp.bfloat16), (("zslab", 1),), 1).astype(planes_now.dtype)
    misfit = (
        cone_here[0][:, :, None] * padded[:, :-2]
        + cone_here[1][:, :, None] * padded[:, 1:-1]
        + cone_here[2][:, :, None] * padded[:, 2:]
        - measured
    )
    update = scatter_rows(make_term(misfit))
    coefficients = (first_own.astype(jnp.float32) - step_scale * update).astype(jnp.bfloat16)
    return (coefficients, misfit)


def solution(mesh):
    placed = (
        P("angle", "zslab", None),
        P(),
        P("angle"),
        P("angle"),
        P("angle", None, None),
        P("angle", None, None),
        P(None, "angle", None),
    )
    return jax.shard_map(
        local,
        mesh=mesh,
        in_specs=placed,
        out_specs=(P("angle", None, "zslab", None), P("angle", "zslab", None)),
        check_vma=False,
    )
```

profile of v0, /device:TPU:4, one launch (start us, length us, event | category | flops | bytes accessed | tf_op | source)
XLA Modules:
  0.0 1161.7 jit_solution(14098871874555175160)
XLA Ops:
  20.9 17.2 %while.40 = (s32[]{:T(128)}, f32[64,8,1,2048]{3,1,2,0:T(8,128)}, s32[4,64,16]{2,1,0:T(8,128)S(1)}, bf16[4,8,1,16,128]{4,3,1,0,2:T(8,128)(2,1)S(1)}, bf16[4,128,2...) while((s32[]{:T(128)}, f32[64,8,1,2048]{3,1,2,0:T(8,128)}, ...), condition=%wide.region_1.2_spmd, body=%wide.region_0.1_spmd.sunk | while | flops 606111744 | bytes 14053523 | solution.py:118
  38.1 325.8 %reduce-scatter.3.cloned.1.call-done = f32[1,8,1,2048]{3,1,2,0:T(8,128)} async-done(((f32[64,8,1,2048]{3,1,2,0:T(8,128)}), f32[1,8,1,2048]{3,1,2,0:T(8,128)}) %reduce-scatter.3.cloned.1.call-update) | async-done | bytes 65552 | tf_op jit(solution)/shard_map/reduce_scatter | solution.py:123
  365.4 294.5 %all-gather.2.cloned.1.call-done = bf16[64,8,1,2048]{3,1,2,0:T(8,128)(2,1)} async-done(((bf16[1,8,1,2048]{3,1,2,0:T(8,128)(2,1)}), bf16[64,8,1,2048]{3,1,2,0:T(8,128)(2,1)}) %all-gather.2.cloned.1.call-update) | async-done | bytes 2097168 | tf_op jit(solution)/shard_map/all_gather | solution.py:133
  659.9 132.7 %while.42 = (s32[]{:T(128)}, f32[4,8,1,16,128]{4,3,1,0,2:T(8,128)S(1)}, bf16[64,8,1,2048]{3,1,0,2:T(8,128)(2,1)}, bf16[4,128,256]{2,1,0:T(8,128)(2,1)S(1)}, s32[...) while((s32[]{:T(128)}, f32[4,8,1,16,128]{4,3,1,0,2:T(8,128)S(1)}, ...), condition=%wide.region_4.5_spmd.clone, body=%wide.region_3.4_spmd.clone.sunk | while | flops 679741440 | bytes 44863640 | solution.py:143
  661.1 4.5 convolution_bitcast_fusion.2
  665.5 10.8 reshape.226
  676.4 8.3 fusion.96
  684.7 8.4 fusion.97
  694.2 4.5 convolution_bitcast_fusion.2
  698.6 10.8 reshape.226
  709.5 8.3 fusion.96
  717.8 8.4 fusion.97
  727.3 4.5 convolution_bitcast_fusion.2
  731.7 10.8 reshape.226
  742.6 8.3 fusion.96
  750.9 8.4 fusion.97
  764.9 10.8 reshape.226
  775.7 8.3 fusion.96
  784.0 8.4 fusion.97
  794.9 5.1 collective-permute-start.3
  801.7 5.2 collective-permute-start.4
  808.8 5.2 collective-permute-done.5
  816.9 17.2 %while.41 = (s32[]{:T(128)}, f32[64,8,1,2048]{3,1,2,0:T(8,128)}, s32[4,64,16]{2,1,0:T(8,128)S(1)}, bf16[4,8,1,16,128]{4,3,1,0,2:T(8,128)(2,1)S(1)}, bf16[4,128,2...) while((s32[]{:T(128)}, f32[64,8,1,2048]{3,1,2,0:T(8,128)}, ...), condition=%wide.region_6.7_spmd, body=%wide.region_5.6_spmd.sunk | while | flops 606111744 | bytes 14053523 | solution.py:118
  834.8 318.9 %reduce-scatter.5.cloned.1.call-done = f32[1,8,1,2048]{3,1,2,0:T(8,128)} async-done(((f32[64,8,1,2048]{3,1,2,0:T(8,128)}), f32[1,8,1,2048]{3,1,2,0:T(8,128)}) %reduce-scatter.5.cloned.1.call-update) | async-done | bytes 65552 | tf_op jit(solution)/shard_map/reduce_scatter | solution.py:123
  (111 shorter events, 69.4 us)
Async XLA Ops:
  7.2 6.7 copy-start
  7.2 356.7 %reduce-scatter.3.cloned.1.call-start = ((), (), s32[]{:S(2)}) async-start(), calls=%async_computation.2 | async-start | bytes 4259840 | tf_op jit(solution)/shard_map/reduce_scatter | solution.py:123
  8.1 9.0 collective-permute-start
  10.0 7.1 collective-permute-start.1
  38.1 621.9 %copy-start.1 = (bf16[4,128,256]{2,1,0:T(8,128)(2,1)S(1)}, bf16[4,128,256]{2,1,0:T(8,128)(2,1)}, u32[]{:S(2)}) copy-start(bf16[4,128,256]{2,1,0:T(8,128)(2,1)} %param.17) | copy-start | bytes 786436
  38.1 621.9 %copy-start.2 = (s32[4,64,16]{1,2,0:T(8,128)S(1)}, s32[4,64,16]{1,2,0:T(8,128)}, u32[]{:S(2)}) copy-start(s32[4,64,16]{1,2,0:T(8,128)} %param.18) | copy-start | bytes 49156
  38.1 621.8 %all-gather.2.cloned.1.call-start = ((), (), s32[]{:S(2)}) async-start(), calls=%async_computation.3 | async-start | bytes 2129920 | tf_op jit(solution)/shard_map/all_gather | solution.py:133
  365.4 788.3 %reduce-scatter.5.cloned.1.call-start = ((), (), s32[]{:S(2)}) async-start(), calls=%async_computation.4 | async-start | bytes 4259840 | tf_op jit(solution)/shard_map/reduce_scatter | solution.py:123
  659.9 141.7 %copy-start.3 = (f32[8,1,2048]{2,1,0:T(1,128)S(1)}, f32[8,1,2048]{2,1,0:T(1,128)}, u32[]{:S(2)}) copy-start(f32[8,1,2048]{2,1,0:T(1,128)} %param.13) | copy-start | bytes 196612
  792.9 7.8 collective-permute-start.2
  794.9 6.7 collective-permute-start.3
  801.7 7.1 collective-permute-start.4
  806.9 7.1 collective-permute-start.5
  834.1 319.6 %copy-start.4 = (f32[1,8,1,2048]{3,1,2,0:T(8,128)S(1)}, f32[1,8,1,2048]{3,1,2,0:T(8,128)}, u32[]{:S(2)}) copy-start(f32[1,8,1,2048]{3,1,2,0:T(8,128)} %reduce-scatter.3.cloned.1.call-done) | copy-start | bytes 196612
Sparse Core Ops, SparseCore 0:
  38.2 325.6 reduce-scatter.2
  366.4 293.4 all-gather.1
  834.2 319.3 reduce-scatter.4
where the time goes:
time: 1160 us
  waiting for transfers between devices  945 us (81%)
  matrix products  110 us (9%)
  local copies, waits for them, and re-layouts  69.5 us (6%)
  starting transfers between devices  18.6 us (2%)
  between operations  13.9 us (1%)
    reduce_scatter x2, waiting for transfers between devices, scatter_rows(): lax.psum_scatter(term(jnp.int32(0), ROWS_DEV * lax.axis_size('angle')), '...  645 us
    all_gather x1, waiting for transfers between devices, local(): row_piece = lax.all_gather(first_own, 'angle', axis=0, tiled=True)  294 us
    reshape x4, local copies, waits for them, and re-layouts, project_block(): response.reshape(block, image_width // tile_size, angles_here, basis_coun...  43 us
    dot_general x4, matrix products, land_parts(): jnp.einsum('ayihj,yiakzhc->akzjc', landing, upper, preferred_element_type...  33.5 us
    dot_general x4, matrix products, land_parts(): jnp.einsum('ayihj,yiakzhc->akzjc', landing, lower, preferred_element_type...  33.3 us
  transfers between devices with their start and end apart: 9, of which 5 were waited for; matrix products, arithmetic and copies ran while one was open for 1% of the time, Pallas kernels for 0%

commit v1 on v0

v1 whole, which is shorter than its diff:
```python
import functools

import jax
import jax.numpy as jnp
from jax import lax
from jax.experimental import pallas as pl
from jax.experimental.pallas import tpu as pltpu
from jax.sharding import PartitionSpec as P

GRIDS = {64: (4, 8, 2), 8: (2, 2, 2)}
MESH = pl.DeviceIdType.MESH
STEP = 0.4
TILE = 128
BASIS = 8
PROJ = 8
ANG = 4
TILES = 16
SPLIT_PHI = True
f32, bf16, i32 = jnp.float32, jnp.bfloat16, jnp.int32
SLAB_OFFS = (-2, 2, -1, 1)

NN = (((1,), (0,)), ((), ()))
NT = (((1,), (1,)), ((), ()))


def mm(a, b, dims=NN):
    return lax.dot_general(a, b, dims, preferred_element_type=f32)


def split(value):
    high = value.astype(bf16)
    return high, (value - high.astype(f32)).astype(bf16)


def iota(shape, dim):
    return lax.broadcasted_iota(i32, shape, dim)


def kernel(
    grid, slabs,
    meas_ref, basis_ref, frame_ref, slot_ref, w_ref, off_ref, cone_ref,
    coef_ref, misfit_ref,
    meta_send, meta_recv, x_ref, m_ref, ml_ref, halo_ref, plane_ref, planes_ref,
    r1_ref, r2_ref, p1_send, p1_recv, p2_send, p2_recv, first_ref, s_send, s_recv,
    a_ss, a_rs, b_ss, b_rs, z_ss, z_rs,
):
    ny, nz, nx = grid
    na, nb = nz, ny * nx
    slab = lax.axis_index("zslab")
    place = lax.axis_index("angle")
    my_x = place % nx
    alpha = (place // nx) % nz
    my_y = place // (nx * nz)
    beta = my_y * nx + my_x

    a_steps = sorted(range(1, na), key=lambda d: -min(d, na - d))
    b_steps = sorted(
        [(dy, dx) for dy in range(ny) for dx in range(nx) if dy or dx],
        key=lambda s: -(min(s[0], ny - s[0]) + s[1]),
    )

    def a_at(step):
        return lax.rem(alpha + step + na, na)

    def a_device(step):
        return my_y * (nz * nx) + a_at(step) * nx + my_x

    def b_at(step):
        return lax.rem(my_y + step[0] + ny, ny) * nx + lax.rem(my_x + step[1] + nx, nx)

    def b_device(step):
        other = b_at(step)
        return (other // nx) * (nz * nx) + alpha * nx + other % nx

    def a_copy(phase, n, src, dst):
        return pltpu.make_async_remote_copy(
            src_ref=src, dst_ref=dst, send_sem=a_ss.at[phase, n], recv_sem=a_rs.at[phase, n],
            device_id={"angle": a_device(a_steps[n])}, device_id_type=MESH,
        )

    def b_copy(phase, n, src, dst):
        return pltpu.make_async_remote_copy(
            src_ref=src, dst_ref=dst, send_sem=b_ss.at[phase, n], recv_sem=b_rs.at[phase, n],
            device_id={"angle": b_device(b_steps[n])}, device_id_type=MESH,
        )

    def z_valid(step):
        return jnp.logical_and(slab + step >= 0, slab + step < slabs)

    def z_index(step):
        return SLAB_OFFS.index(step)

    def z_copy(phase, step, src, dst_of):
        back_slot = z_index(-step)
        return pltpu.make_async_remote_copy(
            src_ref=src, dst_ref=dst_of(back_slot), send_sem=z_ss.at[phase, z_index(step)],
            recv_sem=z_rs.at[phase, back_slot],
            device_id={"zslab": slab + step}, device_id_type=MESH,
        )

    def z_arrival(phase, step, src, dst_of):
        slot = z_index(step)
        return pltpu.make_async_remote_copy(
            src_ref=src, dst_ref=dst_of(slot), send_sem=z_ss.at[phase, slot],
            recv_sem=z_rs.at[phase, slot],
            device_id={"zslab": slab + step}, device_id_type=MESH,
        )

    barrier = pltpu.get_barrier_semaphore()
    for step in a_steps:
        pl.semaphore_signal(barrier, inc=1, device_id={"angle": a_device(step)}, device_id_type=MESH)
    for step in b_steps:
        pl.semaphore_signal(barrier, inc=1, device_id={"angle": b_device(step)}, device_id_type=MESH)
    for step in range(1, slabs):
        pl.semaphore_signal(
            barrier, inc=1, device_id={"zslab": lax.rem(slab + step, slabs)}, device_id_type=MESH
        )

    slots = [slot_ref[p] for p in range(PROJ)]
    rows = iota((PROJ * TILES, ANG * TILES), 0)
    cols = iota((PROJ * TILES, ANG * TILES), 1)
    slot_rows = jnp.concatenate(
        [jnp.full((TILES, ANG * TILES), slots[p], i32) for p in range(PROJ)], axis=0
    )
    pick = jnp.logical_and((rows & (TILES - 1)) == (cols & (TILES - 1)), slot_rows == (cols >> 4))
    offs = off_ref[...].reshape(ANG * TILES, na * nb).astype(f32).astype(bf16)
    offs_p = mm(pick.astype(f32).astype(bf16), offs)
    order = iota((na * nb, na * nb), 0)
    o_alpha, o_beta = order // nb, order % nb
    image_row = (o_beta // nx) * (nz * nx) + o_alpha * nx + o_beta % nx
    permute = (image_row == iota((na * nb, na * nb), 1)).astype(f32).astype(bf16)
    offs_sent = mm(permute, offs_p.astype(bf16), NT)

    lane_p = iota((32, TILE), 1) >> 4
    frames = jnp.zeros((32, TILE), i32)
    for p in range(PROJ):
        frames = jnp.where(lane_p == p, frame_ref[p], frames)
    hot = (frames == iota((32, TILE), 0)).astype(f32)
    phi = lax.dot_general(
        basis_ref[...], hot, NN, precision=lax.Precision.HIGHEST, preferred_element_type=f32
    )
    for a in range(na):
        meta_send[a, 0:nb, :] = offs_sent[a * nb:(a + 1) * nb]
        meta_send[a, 8:16, :] = phi
    meta_recv[alpha] = meta_send[alpha]

    for step in (-2, 2, -1, 1):
        @pl.when(jnp.logical_not(z_valid(step)))
        def _():
            planes_ref[z_index(step)] = jnp.zeros((TILE, TILE), bf16)
            if abs(step) == 1:
                halo_ref[z_index(step) - 2] = jnp.zeros((TILE, TILE), f32)

    pl.semaphore_wait(barrier, len(a_steps) + len(b_steps) + slabs - 1)

    halo_at = lambda slot: halo_ref.at[slot - 2]
    planes_at = lambda slot: planes_ref.at[slot]
    for step in (-1, 1):
        @pl.when(z_valid(step))
        def _():
            z_copy(0, step, meas_ref, halo_at).start()
    for n, step in enumerate(a_steps):
        a_copy(0, n, meta_send.at[a_at(step)], meta_recv.at[alpha]).start()

    def cone(kind, step, p):
        at = jnp.clip(slab + step, 0, slabs - 1)
        return cone_ref[kind, at, p]

    def cone_masked(kind, step, p):
        return jnp.where(z_valid(step), cone(kind, step, p), 0.0)

    def part(value, p):
        return value[p * TILES:(p + 1) * TILES]

    def back_of(below, here, above):
        return jnp.concatenate([
            cone_masked(0, 1, p) * part(above, p) + cone(1, 0, p) * part(here, p)
            + cone_masked(2, -1, p) * part(below, p)
            for p in range(PROJ)
        ], axis=0)

    def shift_up(value):
        return jnp.concatenate([value[1:], value[:1]], axis=0)

    def shift_down(value):
        return jnp.concatenate([value[-1:], value[:-1]], axis=0)

    def responses(back):
        window = jnp.concatenate([back, shift_up(back)], axis=1)
        high, low = split(window)
        weights = w_ref[...].reshape(ANG * TILE, 2 * TILE)
        every = mm(high, weights, NT) + mm(low, weights, NT)
        picked = []
        for p in range(PROJ):
            block = part(every, p)
            own = jnp.zeros((TILES, TILE), f32)
            for a in range(ANG):
                own = jnp.where(slots[p] == a, block[:, a * TILE:(a + 1) * TILE], own)
            picked.append(own)
        return jnp.concatenate(picked, axis=0)

    def send_responses(phase, r_ref, back):
        r_ref[alpha] = responses(back).astype(bf16)
        for n in range(na - 1):
            a_copy(phase, n, r_ref.at[alpha], r_ref.at[alpha]).start()

    def a_wait(phase, ref_of):
        for n, step in enumerate(a_steps):
            ref = ref_of(n, a_at(-step))
            a_copy(phase, n, ref, ref).wait_recv()

    def b_wait(phase, ref_of):
        for n, step in enumerate(b_steps):
            ref = ref_of(n, b_at((-step[0], -step[1])))
            b_copy(phase, n, ref, ref).wait_recv()

    for step in (-1, 1):
        @pl.when(z_valid(step))
        def _():
            z_arrival(0, step, meas_ref, halo_at).wait_recv()
    measured = meas_ref[...]
    below, above = halo_ref[0], halo_ref[1]
    send_responses(1, r1_ref, back_of(below, measured, above))

    a_wait(0, lambda n, at: meta_recv.at[at])
    near = jnp.concatenate([meta_recv[a, 0:nb, :] for a in range(na)], axis=0).astype(bf16)
    e_row, e_col = iota((TILE, TILE), 0), iota((TILE, TILE), 1)
    same = (e_row >> 4) == (e_col >> 4)
    for i in range(TILES):
        expand = jnp.logical_and(same, (e_row & (TILES - 1)) == i).astype(f32).astype(bf16)
        x_ref[i] = mm(near, expand)
    tile_lane = (iota((BASIS, TILE), 1) & (TILES - 1)).astype(f32)
    phi_high, phi_low = [], []
    for a in range(na):
        value = meta_recv[a, 8:16, :]
        high = value.astype(bf16).astype(f32)
        phi_high.append(high)
        phi_low.append(value - high)

    def build(b, carry):
        for pair in range(TILES // 2):
            for a in range(na):
                high, low = [], []
                for i in (2 * pair, 2 * pair + 1):
                    line = x_ref[i, pl.ds(a * nb + b, 1), :]
                    hit = jnp.broadcast_to(line, (BASIS, TILE)) == tile_lane
                    high.append(jnp.where(hit, phi_high[a], 0.0))
                    low.append(jnp.where(hit, phi_low[a], 0.0))
                at = pl.ds(pl.multiple_of(b * TILE + pair * 16, 16), 16)
                m_ref[at, a * TILE:(a + 1) * TILE] = jnp.concatenate(high, axis=0).astype(bf16)
                if SPLIT_PHI:
                    ml_ref[at, a * TILE:(a + 1) * TILE] = jnp.concatenate(low, axis=0).astype(bf16)
        return carry

    lax.fori_loop(0, nb, build, 0)

    def scatter_gradient(phase, r_ref, p_send, p_recv):
        gathered = r_ref[...].reshape(na * TILE, TILE)

        def rows_of(b):
            at = pl.ds(pl.multiple_of(b * TILE, TILE), TILE)
            value = mm(m_ref[at, :], gathered)
            if SPLIT_PHI:
                value = value + mm(ml_ref[at, :], gathered)
            return value

        for n, step in enumerate(b_steps):
            p_send[n] = rows_of(b_at(step)).astype(bf16)
            b_copy(phase, n, p_send.at[n], p_recv.at[n]).start()
        total = rows_of(beta)
        b_wait(phase, lambda n, at: p_recv.at[n])
        for n in range(nb - 1):
            total = total + p_recv[n].astype(f32)
        return total

    a_wait(1, lambda n, at: r1_ref.at[at])
    first = (STEP * scatter_gradient(0, r1_ref, p1_send, p1_recv)).astype(bf16)
    first32 = first.astype(f32)

    first_ref[beta] = first32.T.astype(bf16)
    for n in range(nb - 1):
        b_copy(1, n, first_ref.at[beta], first_ref.at[beta]).start()
    b_wait(1, lambda n, at: first_ref.at[at])
    fields = jnp.concatenate([first_ref[b] for b in range(nb)], axis=1)

    def sums_of(a):
        at = pl.ds(pl.multiple_of(a * TILE, TILE), TILE)
        value = mm(fields, m_ref[:, at])
        if SPLIT_PHI:
            value = value + mm(fields, ml_ref[:, at])
        return value

    for n, step in enumerate(a_steps):
        s_send[n] = sums_of(a_at(step)).astype(bf16)
        a_copy(2, n, s_send.at[n], s_recv.at[n]).start()
    sums = sums_of(alpha)
    a_wait(2, lambda n, at: s_recv.at[n])
    for n in range(na - 1):
        sums = sums + s_recv[n].astype(f32)
    sums = sums.T
    zero = jnp.zeros((TILES, TILE), f32)
    masked = jnp.concatenate([
        jnp.concatenate([jnp.where(slots[p] == a, part(sums, p), zero) for a in range(ANG)], axis=1)
        for p in range(PROJ)
    ], axis=0)
    high, low = split(masked)
    weights = w_ref[...].reshape(ANG * TILE, 2 * TILE)
    landed = mm(high, weights) + mm(low, weights)
    plane = landed[:, :TILE] + shift_down(landed[:, TILE:])
    plane_ref[...] = plane.astype(bf16)
    for step in SLAB_OFFS:
        @pl.when(z_valid(step))
        def _():
            z_copy(1, step, plane_ref, planes_at).start()
    for step in SLAB_OFFS:
        @pl.when(z_valid(step))
        def _():
            z_arrival(1, step, plane_ref, planes_at).wait_recv()
    planes = {step: planes_ref[z_index(step)].astype(f32) for step in SLAB_OFFS}
    planes[0] = plane
    seen = {-1: below, 0: measured, 1: above}

    def misfit_at(v):
        return jnp.concatenate([
            cone(0, v, p) * part(planes[v - 1], p) + cone(1, v, p) * part(planes[v], p)
            + cone(2, v, p) * part(planes[v + 1], p) - part(seen[v], p)
            for p in range(PROJ)
        ], axis=0)

    misfit = misfit_at(0)
    misfit_ref[...] = misfit

    send_responses(3, r2_ref, back_of(misfit_at(-1), misfit, misfit_at(1)))
    a_wait(3, lambda n, at: r2_ref.at[at])
    update = scatter_gradient(2, r2_ref, p2_send, p2_recv)
    coefficients = (first32 - STEP * update).astype(bf16)
    coef_ref[...] = jnp.concatenate(
        [coefficients[i * BASIS:(i + 1) * BASIS] for i in range(TILES)], axis=1
    )

    for n in range(na - 1):
        a_copy(0, n, meta_send.at[0], meta_recv.at[0]).wait_send()
        a_copy(1, n, r1_ref.at[0], r1_ref.at[0]).wait_send()
        a_copy(2, n, s_send.at[n], s_recv.at[n]).wait_send()
        a_copy(3, n, r2_ref.at[0], r2_ref.at[0]).wait_send()
    for n in range(nb - 1):
        b_copy(0, n, p1_send.at[n], p1_recv.at[n]).wait_send()
        b_copy(1, n, first_ref.at[0], first_ref.at[0]).wait_send()
        b_copy(2, n, p2_send.at[n], p2_recv.at[n]).wait_send()
    for step in SLAB_OFFS:
        @pl.when(z_valid(step))
        def _():
            if abs(step) == 1:
                z_copy(0, step, meas_ref, halo_at).wait_send()
            z_copy(1, step, plane_ref, planes_at).wait_send()


def local(grid, slabs, measured, basis_time, frame_index, angle_slot, proj_weights, tile_offsets, cone_weights):
    ny, nz, nx = grid
    na, nb = nz, ny * nx
    block = (TILE, TILE)
    vmem = pl.BlockSpec(memory_space=pltpu.VMEM)
    smem = pl.BlockSpec(memory_space=pltpu.SMEM)
    coefficients, misfit = pl.pallas_call(
        functools.partial(kernel, grid, slabs),
        out_shape=(
            jax.ShapeDtypeStruct((BASIS, TILES * TILE), bf16),
            jax.ShapeDtypeStruct(block, f32),
        ),
        in_specs=[vmem, vmem, smem, smem, vmem, vmem, smem],
        out_specs=(vmem, vmem),
        scratch_shapes=[
            pltpu.VMEM((na, 16, TILE), f32),
            pltpu.VMEM((na, 16, TILE), f32),
            pltpu.VMEM((TILES, na * nb, TILE), f32),
            pltpu.VMEM((nb * TILE, na * TILE), bf16),
            pltpu.VMEM((nb * TILE, na * TILE), bf16),
            pltpu.VMEM((2,) + block, f32),
            pltpu.VMEM(block, bf16),
            pltpu.VMEM((4,) + block, bf16),
            pltpu.VMEM((na,) + block, bf16),
            pltpu.VMEM((na,) + block, bf16),
            pltpu.VMEM((nb - 1,) + block, bf16),
            pltpu.VMEM((nb - 1,) + block, bf16),
            pltpu.VMEM((nb - 1,) + block, bf16),
            pltpu.VMEM((nb - 1,) + block, bf16),
            pltpu.VMEM((nb,) + block, bf16),
            pltpu.VMEM((na - 1,) + block, bf16),
            pltpu.VMEM((na - 1,) + block, bf16),
            pltpu.SemaphoreType.DMA((4, na - 1)),
            pltpu.SemaphoreType.DMA((4, na - 1)),
            pltpu.SemaphoreType.DMA((3, nb - 1)),
            pltpu.SemaphoreType.DMA((3, nb - 1)),
            pltpu.SemaphoreType.DMA((2, 4)),
            pltpu.SemaphoreType.DMA((2, 4)),
        ],
        compiler_params=pltpu.CompilerParams(
            collective_id=0, has_side_effects=True, vmem_limit_bytes=40 * 1024 * 1024
        ),
        name="two_gradients",
    )(
        measured.reshape(block),
        basis_time.T,
        frame_index,
        angle_slot,
        proj_weights,
        tile_offsets.transpose(0, 2, 1),
        cone_weights.transpose(0, 2, 1),
    )
    return (
        coefficients.reshape(1, BASIS, 1, TILES * TILE),
        misfit.reshape(PROJ, 1, TILES * TILE),
    )


def solution(mesh):
    placed = (
        P("angle", "zslab", None),
        P(),
        P("angle"),
        P("angle"),
        P("angle", None, None),
        P("angle", None, None),
        P(None, "angle", None),
    )
    grid = GRIDS[mesh.shape["angle"]]
    return jax.shard_map(
        functools.partial(local, grid, mesh.shape["zslab"]),
        mesh=mesh,
        in_specs=placed,
        out_specs=(P("angle", None, "zslab", None), P("angle", "zslab", None)),
        check_vma=False,
    )
```

time: 1160 us -> 64.3 us (0.06)
  the two profiles are of different devices: /device:TPU:4 before, /device:TPU:1 now
where the time goes in v1:
time: 64.3 us; the launch traced here: 64 us
  Pallas kernels  58.2 us (91%)
  local copies, waits for them, and re-layouts  5.15 us (8%)
  between operations  0.67 us (1%)
    pallas_call x1, Pallas kernels, local(): pl.pallas_call(functools.partial(kernel, grid, slabs), out_shape=(jax.Sha...  58.2 us
    unnamed x16, local copies, waits for them, and re-layouts  5.15 us

profile of v1, /device:TPU:1, one launch (start us, length us, event | category | flops | bytes accessed | tf_op | source)
XLA Modules:
  0.0 64.0 jit_solution(4848740826697773706)
XLA Ops:
  0.6 0.0 copy-start.3
  0.6 0.0 copy-start.5
  0.7 0.0 copy-start.6
  0.7 0.7 %copy-done.3 = f32[3,8,4]{1,2,0:T(4,128)S(1)} copy-done((f32[3,8,4]{1,2,0:T(4,128)S(1)}, f32[3,8,4]{1,2,0:T(4,128)}, u32[]{:S(2)}) %copy-start.3) | copy-done | bytes 408
  1.3 0.0 copy-done.5
  1.3 0.0 copy-done.6
  1.3 0.0 copy-start
  1.3 0.9 %copy-done = bf16[4,128,256]{2,1,0:T(8,128)(2,1)S(1)} copy-done((bf16[4,128,256]{2,1,0:T(8,128)(2,1)S(1)}, bf16[4,128,256]{2,1,0:T(8,128)(2,1)}, u32[]{:S(2)}) %copy-start) | copy-done | bytes 262168
  2.3 0.0 copy-start.1
  2.3 0.8 %copy-done.1 = f32[8,1,2048]{2,1,0:T(1,128)S(1)} copy-done((f32[8,1,2048]{2,1,0:T(1,128)S(1)}, f32[8,1,2048]{2,1,0:T(1,128)}, u32[]{:S(2)}) %copy-start.1) | copy-done | bytes 65560
  3.1 0.0 copy-start.2
  3.1 0.8 %copy-done.2 = s32[4,64,16]{1,2,0:T(8,128)S(1)} copy-done((s32[4,64,16]{1,2,0:T(8,128)S(1)}, s32[4,64,16]{1,2,0:T(8,128)}, u32[]{:S(2)}) %copy-start.2) | copy-done | bytes 16408
  3.9 0.0 copy-start.4
  3.9 0.7 %copy-done.4 = f32[32,8]{0,1:T(8,128)S(1)} copy-done((f32[32,8]{0,1:T(8,128)S(1)}, f32[32,8]{0,1:T(8,128)}, u32[]{:S(2)}) %copy-start.4) | copy-done | bytes 1048
  4.6 58.2 %two_gradients.1 = (bf16[8,2048]{1,0:T(8,128)(2,1)S(1)}, f32[128,128]{1,0:T(8,128)S(1)}) custom-call(f32[128,128]{1,0:T(8,128)S(1)} %bitcast.7, f32[8,32]{1,0:T(8,128)S(1)} %bitcast.11, s32[8]{0:T(128)S(1)} %copy-done.5, s32[8]{0:T(128)S(1)} %copy-done.6, bf16[4,128,256]{2,1,0:T(8,128)(2,1)S(1)} %copy-done, s32[4,16,64]{2,1,0:T(8,128)S(1)} %bitcast.8, ...), custom_call_target="tpu_custom_call" | custom-call | tf_op jit(solution)/shard_map/two_gradients/pallas_call | solution.py:364
  62.8 0.6 copy.12
  63.4 0.6 copy.13
Async XLA Ops:
  0.6 0.7 %copy-start.3 = (f32[3,8,4]{1,2,0:T(4,128)S(1)}, f32[3,8,4]{1,2,0:T(4,128)}, u32[]{:S(2)}) copy-start(f32[3,8,4]{1,2,0:T(4,128)} %param.13) | copy-start | bytes 1156
  0.6 0.7 %copy-start.5 = (s32[8]{0:T(128)S(1)}, s32[8]{0:T(128)}, u32[]{:S(2)}) copy-start(s32[8]{0:T(128)} %frame_ref.1) | copy-start | bytes 100
  0.7 0.7 %copy-start.6 = (s32[8]{0:T(128)S(1)}, s32[8]{0:T(128)}, u32[]{:S(2)}) copy-start(s32[8]{0:T(128)} %slot_ref.1) | copy-start | bytes 100
  1.3 1.0 %copy-start = (bf16[4,128,256]{2,1,0:T(8,128)(2,1)S(1)}, bf16[4,128,256]{2,1,0:T(8,128)(2,1)}, u32[]{:S(2)}) copy-start(bf16[4,128,256]{2,1,0:T(8,128)(2,1)} %w_ref.1) | copy-start | bytes 786436
  2.3 0.8 %copy-start.1 = (f32[8,1,2048]{2,1,0:T(1,128)S(1)}, f32[8,1,2048]{2,1,0:T(1,128)}, u32[]{:S(2)}) copy-start(f32[8,1,2048]{2,1,0:T(1,128)} %param.7) | copy-start | bytes 196612
  3.1 0.8 %copy-start.2 = (s32[4,64,16]{1,2,0:T(8,128)S(1)}, s32[4,64,16]{1,2,0:T(8,128)}, u32[]{:S(2)}) copy-start(s32[4,64,16]{1,2,0:T(8,128)} %param.12) | copy-start | bytes 49156
  3.9 0.7 %copy-start.4 = (f32[32,8]{0,1:T(8,128)S(1)}, f32[32,8]{0,1:T(8,128)}, u32[]{:S(2)}) copy-start(f32[32,8]{0,1:T(8,128)} %param.8) | copy-start | bytes 3076

commit v2 on v1

v2 whole, which is shorter than its diff:
```python
import functools

import jax
import jax.numpy as jnp
from jax import lax
from jax.experimental import pallas as pl
from jax.experimental.pallas import tpu as pltpu
from jax.sharding import PartitionSpec as P

GRIDS = {64: (4, 8, 2), 8: (2, 2, 2)}
MESH = pl.DeviceIdType.MESH
STEP = 0.4
TILE = 128
BASIS = 8
PROJ = 8
ANG = 4
TILES = 16
SPLIT_PHI = False
CHUNKS = 2
UC = TILE // CHUNKS
f32, bf16, i32 = jnp.float32, jnp.bfloat16, jnp.int32
SLAB_OFFS = (-2, 2, -1, 1)

NN = (((1,), (0,)), ((), ()))
NT = (((1,), (1,)), ((), ()))


def mm(a, b, dims=NN):
    return lax.dot_general(a, b, dims, preferred_element_type=f32)


def split(value):
    high = value.astype(bf16)
    return high, (value - high.astype(f32)).astype(bf16)


def iota(shape, dim):
    return lax.broadcasted_iota(i32, shape, dim)


def kernel(
    grid, slabs,
    meas_hbm, basis_hbm, frame_hbm, slot_hbm, w_hbm, off_hbm, cone_hbm,
    coef_ref, misfit_ref,
    meas_ref, basis_ref, frame_ref, slot_ref, w_ref, off_ref, cone_ref, load_sem,
    meta_send, meta_recv, x_ref, m_ref, ml_ref, near_ref, edge_ref, far_ref, plane_ref, planes_ref,
    r1_ref, r2_ref, p1_send, p1_recv, p2_send, p2_recv, first_ref, s_send, s_recv,
    a_ss, a_rs, b_ss, b_rs, z_ss, z_rs, h_ss, h_rs,
):
    ny, nz, nx = grid
    na, nb = nz, ny * nx
    slab = lax.axis_index("zslab")
    place = lax.axis_index("angle")
    my_x = place % nx
    alpha = (place // nx) % nz
    my_y = place // (nx * nz)
    beta = my_y * nx + my_x

    a_steps = sorted(range(1, na), key=lambda d: -min(d, na - d))
    b_steps = sorted(
        [(dy, dx) for dy in range(ny) for dx in range(nx) if dy or dx],
        key=lambda s: -(min(s[0], ny - s[0]) + s[1]),
    )

    def a_at(step):
        return lax.rem(alpha + step + na, na)

    def a_device(step):
        return my_y * (nz * nx) + a_at(step) * nx + my_x

    def b_at(step):
        return lax.rem(my_y + step[0] + ny, ny) * nx + lax.rem(my_x + step[1] + nx, nx)

    def b_device(step):
        other = b_at(step)
        return (other // nx) * (nz * nx) + alpha * nx + other % nx

    def a_copy(phase, c, n, src, dst):
        return pltpu.make_async_remote_copy(
            src_ref=src, dst_ref=dst, send_sem=a_ss.at[phase, c, n], recv_sem=a_rs.at[phase, c, n],
            device_id={"angle": a_device(a_steps[n])}, device_id_type=MESH,
        )

    def b_copy(phase, c, n, src, dst):
        return pltpu.make_async_remote_copy(
            src_ref=src, dst_ref=dst, send_sem=b_ss.at[phase, c, n], recv_sem=b_rs.at[phase, c, n],
            device_id={"angle": b_device(b_steps[n])}, device_id_type=MESH,
        )

    def z_valid(step):
        return jnp.logical_and(slab + step >= 0, slab + step < slabs)

    def z_index(step):
        return SLAB_OFFS.index(step)

    def z_copy(step):
        back_slot = z_index(-step)
        return pltpu.make_async_remote_copy(
            src_ref=plane_ref, dst_ref=planes_ref.at[back_slot], send_sem=z_ss.at[z_index(step)],
            recv_sem=z_rs.at[back_slot], device_id={"zslab": slab + step}, device_id_type=MESH,
        )

    def z_arrival(step):
        slot = z_index(step)
        return pltpu.make_async_remote_copy(
            src_ref=plane_ref, dst_ref=planes_ref.at[slot], send_sem=z_ss.at[slot],
            recv_sem=z_rs.at[slot], device_id={"zslab": slab + step}, device_id_type=MESH,
        )

    odd = slab % 2
    near_copy = pltpu.make_async_remote_copy(
        src_ref=meas_ref, dst_ref=near_ref, send_sem=h_ss.at[0], recv_sem=h_rs.at[0],
        device_id={"zslab": slab + 1 - 2 * odd}, device_id_type=MESH,
    )
    far_step = 2 * odd - 1
    far_valid = jnp.logical_and(slab + far_step >= 0, slab + far_step < slabs)
    far_copy = pltpu.make_async_remote_copy(
        src_ref=edge_ref, dst_ref=far_ref, send_sem=h_ss.at[1], recv_sem=h_rs.at[1],
        device_id={"zslab": slab + far_step}, device_id_type=MESH,
    )

    loads = [
        pltpu.make_async_copy(source, target, load_sem.at[n])
        for n, (source, target) in enumerate([
            (slot_hbm, slot_ref), (off_hbm, off_ref), (frame_hbm, frame_ref), (basis_hbm, basis_ref),
            (meas_hbm, meas_ref), (cone_hbm, cone_ref), (w_hbm, w_ref),
        ])
    ]
    for load in loads:
        load.start()

    sent = []

    def send(copy, valid=None):
        if valid is None:
            copy.start()
        else:
            pl.when(valid)(copy.start)
        sent.append((copy, valid))

    def finish():
        for copy, valid in sent:
            if valid is None:
                copy.wait_send()
            else:
                pl.when(valid)(copy.wait_send)

    barrier = pltpu.get_barrier_semaphore()
    for step in a_steps:
        pl.semaphore_signal(barrier, inc=1, device_id={"angle": a_device(step)}, device_id_type=MESH)
    for step in b_steps:
        pl.semaphore_signal(barrier, inc=1, device_id={"angle": b_device(step)}, device_id_type=MESH)
    for step in range(1, slabs):
        pl.semaphore_signal(
            barrier, inc=1, device_id={"zslab": lax.rem(slab + step, slabs)}, device_id_type=MESH
        )

    for load in loads[:4]:
        load.wait()
    slots = [slot_ref[p] for p in range(PROJ)]
    rows = iota((PROJ * TILES, ANG * TILES), 0)
    cols = iota((PROJ * TILES, ANG * TILES), 1)
    slot_rows = jnp.concatenate(
        [jnp.full((TILES, ANG * TILES), slots[p], i32) for p in range(PROJ)], axis=0
    )
    pick = jnp.logical_and((rows & (TILES - 1)) == (cols & (TILES - 1)), slot_rows == (cols >> 4))
    offs = off_ref[...].reshape(ANG * TILES, na * nb).astype(f32).astype(bf16)
    offs_p = mm(pick.astype(f32).astype(bf16), offs)
    order = iota((na * nb, na * nb), 0)
    o_alpha, o_beta = order // nb, order % nb
    image_row = (o_beta // nx) * (nz * nx) + o_alpha * nx + o_beta % nx
    permute = (image_row == iota((na * nb, na * nb), 1)).astype(f32).astype(bf16)
    offs_sent = mm(permute, offs_p.astype(bf16), NT)

    lane_p = iota((32, TILE), 1) >> 4
    frames = jnp.zeros((32, TILE), i32)
    for p in range(PROJ):
        frames = jnp.where(lane_p == p, frame_ref[p], frames)
    hot = (frames == iota((32, TILE), 0)).astype(f32)
    phi = lax.dot_general(
        basis_ref[...], hot, NN, precision=lax.Precision.HIGHEST, preferred_element_type=f32
    )
    for a in range(na):
        meta_send[a, 0:nb, :] = offs_sent[a * nb:(a + 1) * nb]
        meta_send[a, 8:16, :] = phi
    meta_recv[alpha] = meta_send[alpha]

    for step in SLAB_OFFS:
        @pl.when(jnp.logical_not(z_valid(step)))
        def _():
            planes_ref[z_index(step)] = jnp.zeros((TILE, TILE), bf16)

    @pl.when(jnp.logical_not(far_valid))
    def _():
        far_ref[...] = jnp.zeros((TILE, TILE), bf16)

    for load in loads[4:]:
        load.wait()
    edge_ref[...] = meas_ref[...].astype(bf16)
    pl.semaphore_wait(barrier, len(a_steps) + len(b_steps) + slabs - 1)

    send(far_copy, far_valid)
    send(near_copy)
    for n, step in enumerate(a_steps):
        send(a_copy(0, 0, n, meta_send.at[a_at(step)], meta_recv.at[alpha]))

    def cone(kind, step, p):
        at = jnp.clip(slab + step, 0, slabs - 1)
        return cone_ref[kind, at, p]

    def cone_masked(kind, step, p):
        return jnp.where(z_valid(step), cone(kind, step, p), 0.0)

    def part(value, p):
        return value[p * TILES:(p + 1) * TILES]

    def back_of(below, here, above):
        return jnp.concatenate([
            cone_masked(0, 1, p) * part(above, p) + cone(1, 0, p) * part(here, p)
            + cone_masked(2, -1, p) * part(below, p)
            for p in range(PROJ)
        ], axis=0)

    def shift_up(value):
        return jnp.concatenate([value[1:], value[:1]], axis=0)

    def shift_down(value):
        return jnp.concatenate([value[-1:], value[:-1]], axis=0)

    weights = w_ref[...].reshape(ANG * TILE, 2 * TILE)
    slot_lane = jnp.concatenate(
        [jnp.full((8, TILES), slots[p], i32) for p in range(PROJ)], axis=1
    )

    def send_responses(phase, r_ref, back):
        high, low = split(jnp.concatenate([back, shift_up(back)], axis=1))
        every = mm(weights, high, NT) + mm(weights, low, NT)
        owner = jnp.broadcast_to(slot_lane[:1], (UC, TILE))
        for c in range(CHUNKS):
            own = jnp.zeros((UC, TILE), f32)
            for a in range(ANG):
                at = a * TILE + c * UC
                own = jnp.where(owner == a, every[at:at + UC], own)
            r_ref[c, alpha] = own.astype(bf16)
            for n in range(na - 1):
                send(a_copy(phase, c, n, r_ref.at[c, alpha], r_ref.at[c, alpha]))

    def a_wait(phase, c, ref_of):
        for n, step in enumerate(a_steps):
            ref = ref_of(n, a_at(-step))
            a_copy(phase, c, n, ref, ref).wait_recv()

    def b_wait(phase, c, ref_of):
        for n, step in enumerate(b_steps):
            ref = ref_of(n, b_at((-step[0], -step[1])))
            b_copy(phase, c, n, ref, ref).wait_recv()

    near_copy.wait_recv()
    pl.when(far_valid)(far_copy.wait_recv)
    measured = meas_ref[...]
    beside, beyond = near_ref[...], far_ref[...].astype(f32)
    below = jnp.where(odd == 1, beside, beyond)
    above = jnp.where(odd == 1, beyond, beside)
    send_responses(1, r1_ref, back_of(below, measured, above))

    a_wait(0, 0, lambda n, at: meta_recv.at[at])
    near = jnp.concatenate([meta_recv[a, 0:nb, :] for a in range(na)], axis=0).astype(bf16)
    e_row, e_col = iota((TILE, TILE), 0), iota((TILE, TILE), 1)
    same = (e_row >> 4) == (e_col >> 4)
    for i in range(TILES):
        expand = jnp.logical_and(same, (e_row & (TILES - 1)) == i).astype(f32).astype(bf16)
        x_ref[i] = mm(near, expand)
    tile_lane = (iota((BASIS, TILE), 1) & (TILES - 1)).astype(f32)
    phi_high, phi_low = [], []
    for a in range(na):
        value = meta_recv[a, 8:16, :]
        high = value.astype(bf16).astype(f32)
        phi_high.append(high)
        phi_low.append(value - high)

    def build(b, carry):
        for pair in range(TILES // 2):
            for a in range(na):
                high, low = [], []
                for i in (2 * pair, 2 * pair + 1):
                    line = x_ref[i, pl.ds(a * nb + b, 1), :]
                    hit = jnp.broadcast_to(line, (BASIS, TILE)) == tile_lane
                    high.append(jnp.where(hit, phi_high[a], 0.0))
                    low.append(jnp.where(hit, phi_low[a], 0.0))
                at = pl.ds(pl.multiple_of(b * TILE + pair * 16, 16), 16)
                m_ref[at, a * TILE:(a + 1) * TILE] = jnp.concatenate(high, axis=0).astype(bf16)
                if SPLIT_PHI:
                    ml_ref[at, a * TILE:(a + 1) * TILE] = jnp.concatenate(low, axis=0).astype(bf16)
        return carry

    lax.fori_loop(0, nb, build, 0)

    def wide(ref, c, count):
        return jnp.concatenate([ref[c, j] for j in range(count)], axis=1)

    def scatter_gradient(phase, a_phase, r_ref, p_send, p_recv, use):
        gathered = []

        def rows_of(c, b):
            at = pl.ds(pl.multiple_of(b * TILE, TILE), TILE)
            value = mm(gathered[c], m_ref[at, :], NT)
            if SPLIT_PHI:
                value = value + mm(gathered[c], ml_ref[at, :], NT)
            return value

        for c in range(CHUNKS):
            a_wait(a_phase, c, lambda n, at: r_ref.at[c, at])
            gathered.append(wide(r_ref, c, na))
            for n, step in enumerate(b_steps):
                p_send[c, n] = rows_of(c, b_at(step)).astype(bf16)
                send(b_copy(phase, c, n, p_send.at[c, n], p_recv.at[c, n]))
        own = [rows_of(c, beta) for c in range(CHUNKS)]
        for c in range(CHUNKS):
            b_wait(phase, c, lambda n, at: p_recv.at[c, n])
            total = own[c]
            for n in range(nb - 1):
                total = total + p_recv[c, n].astype(f32)
            use(c, total)

    firsts = []

    def use_first(c, total):
        first = (STEP * total).astype(bf16)
        firsts.append(first.astype(f32))
        first_ref[c, beta] = first
        for n in range(nb - 1):
            send(b_copy(1, c, n, first_ref.at[c, beta], first_ref.at[c, beta]))

    scatter_gradient(0, 1, r1_ref, p1_send, p1_recv, use_first)
    fields = []

    def sums_of(c, a):
        at = pl.ds(pl.multiple_of(a * TILE, TILE), TILE)
        value = mm(fields[c], m_ref[:, at])
        if SPLIT_PHI:
            value = value + mm(fields[c], ml_ref[:, at])
        return value

    for c in range(CHUNKS):
        b_wait(1, c, lambda n, at: first_ref.at[c, at])
        fields.append(wide(first_ref, c, nb))
        for n, step in enumerate(a_steps):
            s_send[c, n] = sums_of(c, a_at(step)).astype(bf16)
            send(a_copy(2, c, n, s_send.at[c, n], s_recv.at[c, n]))
    sums = [sums_of(c, alpha) for c in range(CHUNKS)]
    landed = jnp.zeros((TILE, 2 * TILE), f32)
    for c in range(CHUNKS):
        a_wait(2, c, lambda n, at: s_recv.at[c, n])
        total = sums[c]
        for n in range(na - 1):
            total = total + s_recv[c, n].astype(f32)
        some = jnp.concatenate([w_ref[a, c * UC:(c + 1) * UC, :] for a in range(ANG)], axis=0)
        owner = jnp.broadcast_to(slot_lane[:1], (UC, TILE))
        masked = jnp.concatenate([jnp.where(owner == a, total, 0.0) for a in range(ANG)], axis=0)
        for half in split(masked.T):
            landed = landed + mm(half, some)
    plane = landed[:, :TILE] + shift_down(landed[:, TILE:])
    plane_ref[...] = plane.astype(bf16)
    for step in SLAB_OFFS:
        send(z_copy(step), z_valid(step))
    for step in SLAB_OFFS:
        pl.when(z_valid(step))(z_arrival(step).wait_recv)
    planes = {step: planes_ref[z_index(step)].astype(f32) for step in SLAB_OFFS}
    planes[0] = plane
    seen = {-1: below, 0: measured, 1: above}

    def misfit_at(v):
        return jnp.concatenate([
            cone(0, v, p) * part(planes[v - 1], p) + cone(1, v, p) * part(planes[v], p)
            + cone(2, v, p) * part(planes[v + 1], p) - part(seen[v], p)
            for p in range(PROJ)
        ], axis=0)

    misfit = misfit_at(0)
    misfit_ref[...] = misfit

    send_responses(3, r2_ref, back_of(misfit_at(-1), misfit, misfit_at(1)))
    updates = []
    scatter_gradient(2, 3, r2_ref, p2_send, p2_recv, lambda c, total: updates.append(total))
    rows_now = jnp.concatenate(
        [first - STEP * update for first, update in zip(firsts, updates)], axis=0
    ).T.astype(bf16)
    coef_ref[...] = jnp.concatenate(
        [rows_now[i * BASIS:(i + 1) * BASIS] for i in range(TILES)], axis=1
    )

    finish()


def local(grid, slabs, measured, basis_time, frame_index, angle_slot, proj_weights, tile_offsets, cone_weights):
    ny, nz, nx = grid
    na, nb = nz, ny * nx
    block, chunk = (TILE, TILE), (UC, TILE)
    vmem = pl.BlockSpec(memory_space=pltpu.VMEM)
    hbm = pl.BlockSpec(memory_space=pltpu.HBM)
    coefficients, misfit = pl.pallas_call(
        functools.partial(kernel, grid, slabs),
        out_shape=(
            pltpu.VMEM((BASIS, TILES * TILE), bf16),
            pltpu.VMEM(block, f32),
        ),
        in_specs=[hbm] * 7,
        out_specs=(vmem, vmem),
        scratch_shapes=[
            pltpu.VMEM(block, f32),
            pltpu.VMEM((BASIS, 32), f32),
            pltpu.SMEM((PROJ,), i32),
            pltpu.SMEM((PROJ,), i32),
            pltpu.VMEM((ANG, TILE, 2 * TILE), bf16),
            pltpu.VMEM((ANG, TILES, na * nb), i32),
            pltpu.SMEM((3, slabs, PROJ), f32),
            pltpu.SemaphoreType.DMA((7,)),
            pltpu.VMEM((na, 16, TILE), f32),
            pltpu.VMEM((na, 16, TILE), f32),
            pltpu.VMEM((TILES, na * nb, TILE), f32),
            pltpu.VMEM((nb * TILE, na * TILE), bf16),
            pltpu.VMEM((nb * TILE, na * TILE), bf16),
            pltpu.VMEM(block, f32),
            pltpu.VMEM(block, bf16),
            pltpu.VMEM(block, bf16),
            pltpu.VMEM(block, bf16),
            pltpu.VMEM((4,) + block, bf16),
            pltpu.VMEM((CHUNKS, na) + chunk, bf16),
            pltpu.VMEM((CHUNKS, na) + chunk, bf16),
            pltpu.VMEM((CHUNKS, nb - 1) + chunk, bf16),
            pltpu.VMEM((CHUNKS, nb - 1) + chunk, bf16),
            pltpu.VMEM((CHUNKS, nb - 1) + chunk, bf16),
            pltpu.VMEM((CHUNKS, nb - 1) + chunk, bf16),
            pltpu.VMEM((CHUNKS, nb) + chunk, bf16),
            pltpu.VMEM((CHUNKS, na - 1) + chunk, bf16),
            pltpu.VMEM((CHUNKS, na - 1) + chunk, bf16),
            pltpu.SemaphoreType.DMA((4, CHUNKS, na - 1)),
            pltpu.SemaphoreType.DMA((4, CHUNKS, na - 1)),
            pltpu.SemaphoreType.DMA((3, CHUNKS, nb - 1)),
            pltpu.SemaphoreType.DMA((3, CHUNKS, nb - 1)),
            pltpu.SemaphoreType.DMA((4,)),
            pltpu.SemaphoreType.DMA((4,)),
            pltpu.SemaphoreType.DMA((2,)),
            pltpu.SemaphoreType.DMA((2,)),
        ],
        compiler_params=pltpu.CompilerParams(
            collective_id=0, has_side_effects=True, vmem_limit_bytes=62 * 1000 * 1000
        ),
        name="two_gradients",
    )(
        measured.reshape(block),
        basis_time.T,
        frame_index,
        angle_slot,
        proj_weights,
        tile_offsets.transpose(0, 2, 1),
        cone_weights.transpose(0, 2, 1),
    )
    return (
        coefficients.reshape(1, BASIS, 1, TILES * TILE),
        misfit.reshape(PROJ, 1, TILES * TILE),
    )


def solution(mesh):
    placed = (
        P("angle", "zslab", None),
        P(),
        P("angle"),
        P("angle"),
        P("angle", None, None),
        P("angle", None, None),
        P(None, "angle", None),
    )
    grid = GRIDS[mesh.shape["angle"]]
    return jax.shard_map(
        functools.partial(local, grid, mesh.shape["zslab"]),
        mesh=mesh,
        in_specs=placed,
        out_specs=(P("angle", None, "zslab", None), P("angle", "zslab", None)),
        check_vma=False,
    )
```

time: 64.3 us -> 56.7 us (0.88)
  local copies, waits for them, and re-layouts: 5.15 us -> 1.25 us
  Pallas kernels: 58.2 us -> 54.7 us
    unnamed x16 -> x2, local copies, waits for them, and re-layouts: 5.15 us -> 1.25 us
    pallas_call x1, Pallas kernels: 58.2 us -> 54.7 us  [local(): pl.pallas_call(functools.partial(kernel, grid, slabs), out_shape=(pltpu.V...]
where the time goes in v2:
time: 56.7 us; the launch traced here: 56.6 us
  Pallas kernels  54.7 us (96%)
  local copies, waits for them, and re-layouts  1.25 us (2%)
  between operations  0.64 us (1%)
    pallas_call x1, Pallas kernels, local(): pl.pallas_call(functools.partial(kernel, grid, slabs), out_shape=(pltpu.V...  54.7 us
    unnamed x2, local copies, waits for them, and re-layouts  1.25 us

profile of v2, /device:TPU:1, one launch (start us, length us, event | category | flops | bytes accessed | tf_op | source)
XLA Modules:
  0.0 56.6 jit_solution(17707127760992129831)
XLA Ops:
  0.6 54.7 %two_gradients.1 = (bf16[8,2048]{1,0:T(8,128)(2,1)S(1)}, f32[128,128]{1,0:T(8,128)S(1)}) custom-call(f32[128,128]{1,0:T(8,128)} %bitcast.8, f32[8,32]{1,0:T(8,128)} %bitcast.11, s32[8]{0:T(128)} %frame_hbm.1, s32[8]{0:T(128)} %slot_hbm.1, bf16[4,128,256]{2,1,0:T(8,128)(2,1)} %w_hbm.1, s32[4,16,64]{2,1,0:T(8,128)} %bitcast.9, f32[3,4,8]{2,1,0:T(4,128)} %bitcast.10), custom_call_target="tpu_custom_call" | custom-call | tf_op jit(solution)/shard_map/two_gradients/pallas_call | solution.py:401
  55.4 0.6 %copy.12 = bf16[1,8,1,2048]{3,1,2,0:T(8,128)(2,1)} copy(bf16[1,8,1,2048]{3,1,2,0:T(8,128)(2,1)S(1)} %bitcast.7) | data formatting | bytes 65536
  56.0 0.6 %copy.13 = f32[8,1,2048]{2,1,0:T(1,128)} copy(f32[8,1,2048]{2,1,0:T(1,128)S(1)} %bitcast.6) | data formatting | bytes 131072

commit v3 on v2

--- a/solution.py
+++ b/solution.py
@@ -15,9 +15,8 @@
 PROJ = 8
 ANG = 4
 TILES = 16
-SPLIT_PHI = False
-CHUNKS = 2
-UC = TILE // CHUNKS
+VIEWS = 2
+UC = TILE // VIEWS
 f32, bf16, i32 = jnp.float32, jnp.bfloat16, jnp.int32
 SLAB_OFFS = (-2, 2, -1, 1)
 
@@ -43,9 +42,9 @@
     meas_hbm, basis_hbm, frame_hbm, slot_hbm, w_hbm, off_hbm, cone_hbm,
     coef_ref, misfit_ref,
     meas_ref, basis_ref, frame_ref, slot_ref, w_ref, off_ref, cone_ref, load_sem,
-    meta_send, meta_recv, x_ref, m_ref, ml_ref, near_ref, edge_ref, far_ref, plane_ref, planes_ref,
+    meta_send, meta_recv, x_ref, ma_ref, mb_ref, near_ref, edge_ref, far_ref, plane_ref, planes_ref,
     r1_ref, r2_ref, p1_send, p1_recv, p2_send, p2_recv, first_ref, s_send, s_recv,
-    a_ss, a_rs, b_ss, b_rs, z_ss, z_rs, h_ss, h_rs,
+    g_ss, g_rs, c_ss, c_rs, z_ss, z_rs, h_ss, h_rs,
 ):
     ny, nz, nx = grid
     na, nb = nz, ny * nx
@@ -75,17 +74,25 @@
         other = b_at(step)
         return (other // nx) * (nz * nx) + alpha * nx + other % nx
 
-    def a_copy(phase, c, n, src, dst):
+    groups = (
+        (na, alpha, a_steps, a_at, a_device, lambda step: -step),
+        (nb, beta, b_steps, b_at, b_device, lambda step: (-step[0], -step[1])),
+    )
+    m_refs = (ma_ref, mb_ref)
+
+    def copy(kind, v, phase, n, src, dst):
+        _, _, steps, _, device, _ = groups[(v + kind) % 2]
+        ss, rs = (g_ss, g_rs) if kind == 0 else (c_ss, c_rs)
         return pltpu.make_async_remote_copy(
-            src_ref=src, dst_ref=dst, send_sem=a_ss.at[phase, c, n], recv_sem=a_rs.at[phase, c, n],
-            device_id={"angle": a_device(a_steps[n])}, device_id_type=MESH,
+            src_ref=src, dst_ref=dst, send_sem=ss.at[v, phase, n], recv_sem=rs.at[v, phase, n],
+            device_id={"angle": device(steps[n])}, device_id_type=MESH,
         )
 
-    def b_copy(phase, c, n, src, dst):
-        return pltpu.make_async_remote_copy(
-            src_ref=src, dst_ref=dst, send_sem=b_ss.at[phase, c, n], recv_sem=b_rs.at[phase, c, n],
-            device_id={"angle": b_device(b_steps[n])}, device_id_type=MESH,
-        )
+    def wait_all(kind, v, phase, ref_of):
+        _, _, steps, at, _, opposite = groups[(v + kind) % 2]
+        for n, step in enumerate(steps):
+            ref = ref_of(n, at(opposite(step)))
+            copy(kind, v, phase, n, ref, ref).wait_recv()
 
     def z_valid(step):
         return jnp.logical_and(slab + step >= 0, slab + step < slabs)
@@ -166,11 +173,12 @@
     pick = jnp.logical_and((rows & (TILES - 1)) == (cols & (TILES - 1)), slot_rows == (cols >> 4))
     offs = off_ref[...].reshape(ANG * TILES, na * nb).astype(f32).astype(bf16)
     offs_p = mm(pick.astype(f32).astype(bf16), offs)
+    offs_sent = []
     order = iota((na * nb, na * nb), 0)
-    o_alpha, o_beta = order // nb, order % nb
-    image_row = (o_beta // nx) * (nz * nx) + o_alpha * nx + o_beta % nx
-    permute = (image_row == iota((na * nb, na * nb), 1)).astype(f32).astype(bf16)
-    offs_sent = mm(permute, offs_p.astype(bf16), NT)
+    for o_alpha, o_beta in ((order // nb, order % nb), (order % na, order // na)):
+        image_row = (o_beta // nx) * (nz * nx) + o_alpha * nx + o_beta % nx
+        permute = (image_row == iota((na * nb, na * nb), 1)).astype(f32).astype(bf16)
+        offs_sent.append(mm(permute, offs_p.astype(bf16), NT))
 
     lane_p = iota((32, TILE), 1) >> 4
     frames = jnp.zeros((32, TILE), i32)
@@ -180,10 +188,12 @@
     phi = lax.dot_general(
         basis_ref[...], hot, NN, precision=lax.Precision.HIGHEST, preferred_element_type=f32
     )
-    for a in range(na):
-        meta_send[a, 0:nb, :] = offs_sent[a * nb:(a + 1) * nb]
-        meta_send[a, 8:16, :] = phi
-    meta_recv[alpha] = meta_send[alpha]
+    for v in range(VIEWS):
+        (ng, me, *_), (ns, *_) = groups[v], groups[1 - v]
+        for g in range(ng):
+            meta_send[v, g, 0:ns, :] = offs_sent[v][g * ns:(g + 1) * ns]
+            meta_send[v, g, 8:16, :] = phi
+        meta_recv[v, me] = meta_send[v, me]
 
     for step in SLAB_OFFS:
         @pl.when(jnp.logical_not(z_valid(step)))
@@ -201,8 +211,10 @@
 
     send(far_copy, far_valid)
     send(near_copy)
-    for n, step in enumerate(a_steps):
-        send(a_copy(0, 0, n, meta_send.at[a_at(step)], meta_recv.at[alpha]))
+    for v in range(VIEWS):
+        _, me, steps, at, _, _ = groups[v]
+        for n, step in enumerate(steps):
+            send(copy(0, v, 0, n, meta_send.at[v, at(step)], meta_recv.at[v, me]))
 
     def cone(kind, step, p):
         at = jnp.clip(slab + step, 0, slabs - 1)
@@ -236,24 +248,15 @@
         high, low = split(jnp.concatenate([back, shift_up(back)], axis=1))
         every = mm(weights, high, NT) + mm(weights, low, NT)
         owner = jnp.broadcast_to(slot_lane[:1], (UC, TILE))
-        for c in range(CHUNKS):
+        for v in range(VIEWS):
+            ng, me, *_ = groups[v]
             own = jnp.zeros((UC, TILE), f32)
             for a in range(ANG):
-                at = a * TILE + c * UC
+                at = a * TILE + v * UC
                 own = jnp.where(owner == a, every[at:at + UC], own)
-            r_ref[c, alpha] = own.astype(bf16)
-            for n in range(na - 1):
-                send(a_copy(phase, c, n, r_ref.at[c, alpha], r_ref.at[c, alpha]))
-
-    def a_wait(phase, c, ref_of):
-        for n, step in enumerate(a_steps):
-            ref = ref_of(n, a_at(-step))
-            a_copy(phase, c, n, ref, ref).wait_recv()
-
-    def b_wait(phase, c, ref_of):
-        for n, step in enumerate(b_steps):
-            ref = ref_of(n, b_at((-step[0], -step[1])))
-            b_copy(phase, c, n, ref, ref).wait_recv()
+            r_ref[v, me] = own.astype(bf16)
+            for n in range(ng - 1):
+                send(copy(0, v, phase, n, r_ref.at[v, me], r_ref.at[v, me]))
 
     near_copy.wait_recv()
     pl.when(far_valid)(far_copy.wait_recv)
@@ -263,98 +266,105 @@
     above = jnp.where(odd == 1, beyond, beside)
     send_responses(1, r1_ref, back_of(below, measured, above))
 
-    a_wait(0, 0, lambda n, at: meta_recv.at[at])
-    near = jnp.concatenate([meta_recv[a, 0:nb, :] for a in range(na)], axis=0).astype(bf16)
     e_row, e_col = iota((TILE, TILE), 0), iota((TILE, TILE), 1)
     same = (e_row >> 4) == (e_col >> 4)
-    for i in range(TILES):
-        expand = jnp.logical_and(same, (e_row & (TILES - 1)) == i).astype(f32).astype(bf16)
-        x_ref[i] = mm(near, expand)
     tile_lane = (iota((BASIS, TILE), 1) & (TILES - 1)).astype(f32)
-    phi_high, phi_low = [], []
-    for a in range(na):
-        value = meta_recv[a, 8:16, :]
-        high = value.astype(bf16).astype(f32)
-        phi_high.append(high)
-        phi_low.append(value - high)
-
-    def build(b, carry):
-        for pair in range(TILES // 2):
-            for a in range(na):
-                high, low = [], []
-                for i in (2 * pair, 2 * pair + 1):
-                    line = x_ref[i, pl.ds(a * nb + b, 1), :]
-                    hit = jnp.broadcast_to(line, (BASIS, TILE)) == tile_lane
-                    high.append(jnp.where(hit, phi_high[a], 0.0))
-                    low.append(jnp.where(hit, phi_low[a], 0.0))
-                at = pl.ds(pl.multiple_of(b * TILE + pair * 16, 16), 16)
-                m_ref[at, a * TILE:(a + 1) * TILE] = jnp.concatenate(high, axis=0).astype(bf16)
-                if SPLIT_PHI:
-                    ml_ref[at, a * TILE:(a + 1) * TILE] = jnp.concatenate(low, axis=0).astype(bf16)
-        return carry
-
-    lax.fori_loop(0, nb, build, 0)
+    for v in (1, 0):
+        (ng, *_), (ns, *_), m_ref = groups[v], groups[1 - v], m_refs[v]
+        wait_all(0, v, 0, lambda n, at: meta_recv.at[v, at])
+        near = jnp.concatenate([meta_recv[v, g, 0:ns, :] for g in range(ng)], axis=0).astype(bf16)
+        for i in range(TILES):
+            expand = jnp.logical_and(same, (e_row & (TILES - 1)) == i).astype(f32).astype(bf16)
+            x_ref[v, i] = mm(near, expand)
+        factors = [meta_recv[v, g, 8:16, :] for g in range(ng)]
+
+        def build(b, carry):
+            for pair in range(TILES // 2):
+                for g in range(ng):
+                    lines = []
+                    for i in (2 * pair, 2 * pair + 1):
+                        line = x_ref[v, i, pl.ds(g * ns + b, 1), :]
+                        hit = jnp.broadcast_to(line, (BASIS, TILE)) == tile_lane
+                        lines.append(jnp.where(hit, factors[g], 0.0))
+                    at = pl.ds(pl.multiple_of(b * TILE + pair * 16, 16), 16)
+                    m_ref[at, g * TILE:(g + 1) * TILE] = jnp.concatenate(lines, axis=0).astype(bf16)
+            return carry
+
+        lax.fori_loop(0, ns, build, 0)
 
     def wide(ref, c, count):
         return jnp.concatenate([ref[c, j] for j in range(count)], axis=1)
 
-    def scatter_gradient(phase, a_phase, r_ref, p_send, p_recv, use):
-        gathered = []
-
-        def rows_of(c, b):
-            at = pl.ds(pl.multiple_of(b * TILE, TILE), TILE)
-            value = mm(gathered[c], m_ref[at, :], NT)
-            if SPLIT_PHI:
-                value = value + mm(gathered[c], ml_ref[at, :], NT)
-            return value
-
-        for c in range(CHUNKS):
-            a_wait(a_phase, c, lambda n, at: r_ref.at[c, at])
-            gathered.append(wide(r_ref, c, na))
-            for n, step in enumerate(b_steps):
-                p_send[c, n] = rows_of(c, b_at(step)).astype(bf16)
-                send(b_copy(phase, c, n, p_send.at[c, n], p_recv.at[c, n]))
-        own = [rows_of(c, beta) for c in range(CHUNKS)]
-        for c in range(CHUNKS):
-            b_wait(phase, c, lambda n, at: p_recv.at[c, n])
-            total = own[c]
-            for n in range(nb - 1):
-                total = total + p_recv[c, n].astype(f32)
-            use(c, total)
+    def scatter_gradient(phase, g_phase, r_ref, p_send, p_recv, use):
+        gathered = {}
+
+        def rows_of(v, pair):
+            some = jnp.concatenate(
+                [m_refs[v][pl.ds(pl.multiple_of(b * TILE, TILE), TILE), :] for b in pair], axis=0
+            )
+            value = mm(gathered[v], some, NT)
+            return value[:, :TILE], value[:, TILE:]
+
+        own = {}
+        for v in (1, 0):
+            (ng, *_), (_, _, steps, at_of, _, _) = groups[v], groups[1 - v]
+            wait_all(0, v, g_phase, lambda n, at: r_ref.at[v, at])
+            gathered[v] = wide(r_ref, v, ng)
+            places = [at_of(step) for step in steps] + [groups[1 - v][1]]
+            for n in range(0, len(places), 2):
+                for m, value in zip((n, n + 1), rows_of(v, places[n:n + 2])):
+                    if m == len(steps):
+                        own[v] = value
+                        continue
+                    p_send[v, m] = value.astype(bf16)
+                    send(copy(1, v, phase, m, p_send.at[v, m], p_recv.at[v, m]))
+        for v in (0, 1):
+            wait_all(1, v, phase, lambda n, at: p_recv.at[v, n])
+            total = own[v]
+            for n in range(groups[1 - v][0] - 1):
+                total = total + p_recv[v, n].astype(f32)
+            use(v, total)
 
     firsts = []
 
-    def use_first(c, total):
+    def use_first(v, total):
+        ns, me, *_ = groups[1 - v]
         first = (STEP * total).astype(bf16)
         firsts.append(first.astype(f32))
-        first_ref[c, beta] = first
-        for n in range(nb - 1):
-            send(b_copy(1, c, n, first_ref.at[c, beta], first_ref.at[c, beta]))
+        first_ref[v, me] = first
+        for n in range(ns - 1):
+            send(copy(1, v, 1, n, first_ref.at[v, me], first_ref.at[v, me]))
 
     scatter_gradient(0, 1, r1_ref, p1_send, p1_recv, use_first)
     fields = []
 
-    def sums_of(c, a):
-        at = pl.ds(pl.multiple_of(a * TILE, TILE), TILE)
-        value = mm(fields[c], m_ref[:, at])
-        if SPLIT_PHI:
-            value = value + mm(fields[c], ml_ref[:, at])
-        return value
-
-    for c in range(CHUNKS):
-        b_wait(1, c, lambda n, at: first_ref.at[c, at])
-        fields.append(wide(first_ref, c, nb))
-        for n, step in enumerate(a_steps):
-            s_send[c, n] = sums_of(c, a_at(step)).astype(bf16)
-            send(a_copy(2, c, n, s_send.at[c, n], s_recv.at[c, n]))
-    sums = [sums_of(c, alpha) for c in range(CHUNKS)]
+    def sums_of(v, pair):
+        some = jnp.concatenate(
+            [m_refs[v][:, pl.ds(pl.multiple_of(g * TILE, TILE), TILE)] for g in pair], axis=1
+        )
+        value = mm(fields[v], some)
+        return value[:, :TILE], value[:, TILE:]
+
+    sums = {}
+    for v in (0, 1):
+        (_, _, steps, at_of, _, _), (ns, *_) = groups[v], groups[1 - v]
+        wait_all(1, v, 1, lambda n, at: first_ref.at[v, at])
+        fields.append(wide(first_ref, v, ns))
+        places = [at_of(step) for step in steps] + [groups[v][1]]
+        for n in range(0, len(places), 2):
+            for m, value in zip((n, n + 1), sums_of(v, places[n:n + 2])):
+                if m == len(steps):
+                    sums[v] = value
+                    continue
+                s_send[v, m] = value.astype(bf16)
+                send(copy(0, v, 2, m, s_send.at[v, m], s_recv.at[v, m]))
     landed = jnp.zeros((TILE, 2 * TILE), f32)
-    for c in range(CHUNKS):
-        a_wait(2, c, lambda n, at: s_recv.at[c, n])
-        total = sums[c]
-        for n in range(na - 1):
-            total = total + s_recv[c, n].astype(f32)
-        some = jnp.concatenate([w_ref[a, c * UC:(c + 1) * UC, :] for a in range(ANG)], axis=0)
+    for v in (0, 1):
+        wait_all(0, v, 2, lambda n, at: s_recv.at[v, n])
+        total = sums[v]
+        for n in range(groups[v][0] - 1):
+            total = total + s_recv[v, n].astype(f32)
+        some = jnp.concatenate([w_ref[a, v * UC:(v + 1) * UC, :] for a in range(ANG)], axis=0)
         owner = jnp.broadcast_to(slot_lane[:1], (UC, TILE))
         masked = jnp.concatenate([jnp.where(owner == a, total, 0.0) for a in range(ANG)], axis=0)
         for half in split(masked.T):
@@ -381,7 +391,7 @@
 
     send_responses(3, r2_ref, back_of(misfit_at(-1), misfit, misfit_at(1)))
     updates = []
-    scatter_gradient(2, 3, r2_ref, p2_send, p2_recv, lambda c, total: updates.append(total))
+    scatter_gradient(2, 3, r2_ref, p2_send, p2_recv, lambda v, total: updates.append(total))
     rows_now = jnp.concatenate(
         [first - STEP * update for first, update in zip(firsts, updates)], axis=0
     ).T.astype(bf16)
@@ -395,7 +405,8 @@
 def local(grid, slabs, measured, basis_time, frame_index, angle_slot, proj_weights, tile_offsets, cone_weights):
     ny, nz, nx = grid
     na, nb = nz, ny * nx
-    block, chunk = (TILE, TILE), (UC, TILE)
+    most = max(na, nb)
+    block, blocks = (TILE, TILE), (VIEWS, most, UC, TILE)
     vmem = pl.BlockSpec(memory_space=pltpu.VMEM)
     hbm = pl.BlockSpec(memory_space=pltpu.HBM)
     coefficients, misfit = pl.pallas_call(
@@ -415,29 +426,29 @@
             pltpu.VMEM((ANG, TILES, na * nb), i32),
             pltpu.SMEM((3, slabs, PROJ), f32),
             pltpu.SemaphoreType.DMA((7,)),
-            pltpu.VMEM((na, 16, TILE), f32),
-            pltpu.VMEM((na, 16, TILE), f32),
-            pltpu.VMEM((TILES, na * nb, TILE), f32),
+            pltpu.VMEM((VIEWS, most, 16, TILE), f32),
+            pltpu.VMEM((VIEWS, most, 16, TILE), f32),
+            pltpu.VMEM((VIEWS, TILES, na * nb, TILE), f32),
             pltpu.VMEM((nb * TILE, na * TILE), bf16),
-            pltpu.VMEM((nb * TILE, na * TILE), bf16),
+            pltpu.VMEM((na * TILE, nb * TILE), bf16),
             pltpu.VMEM(block, f32),
             pltpu.VMEM(block, bf16),
             pltpu.VMEM(block, bf16),
             pltpu.VMEM(block, bf16),
             pltpu.VMEM((4,) + block, bf16),
-            pltpu.VMEM((CHUNKS, na) + chunk, bf16),
-            pltpu.VMEM((CHUNKS, na) + chunk, bf16),
-            pltpu.VMEM((CHUNKS, nb - 1) + chunk, bf16),
-            pltpu.VMEM((CHUNKS, nb - 1) + chunk, bf16),
-            pltpu.VMEM((CHUNKS, nb - 1) + chunk, bf16),
-            pltpu.VMEM((CHUNKS, nb - 1) + chunk, bf16),
-            pltpu.VMEM((CHUNKS, nb) + chunk, bf16),
-            pltpu.VMEM((CHUNKS, na - 1) + chunk, bf16),
-            pltpu.VMEM((CHUNKS, na - 1) + chunk, bf16),
-            pltpu.SemaphoreType.DMA((4, CHUNKS, na - 1)),
-            pltpu.SemaphoreType.DMA((4, CHUNKS, na - 1)),
-            pltpu.SemaphoreType.DMA((3, CHUNKS, nb - 1)),
-            pltpu.SemaphoreType.DMA((3, CHUNKS, nb - 1)),
+            pltpu.VMEM(blocks, bf16),
+            pltpu.VMEM(blocks, bf16),
+            pltpu.VMEM(blocks, bf16),
+            pltpu.VMEM(blocks, bf16),
+            pltpu.VMEM(blocks, bf16),
+            pltpu.VMEM(blocks, bf16),
+            pltpu.VMEM(blocks, bf16),
+            pltpu.VMEM(blocks, bf16),
+            pltpu.VMEM(blocks, bf16),
+            pltpu.SemaphoreType.DMA((VIEWS, 4, most - 1)),
+            pltpu.SemaphoreType.DMA((VIEWS, 4, most - 1)),
+            pltpu.SemaphoreType.DMA((VIEWS, 3, most - 1)),
+            pltpu.SemaphoreType.DMA((VIEWS, 3, most - 1)),
             pltpu.SemaphoreType.DMA((4,)),
             pltpu.SemaphoreType.DMA((4,)),
             pltpu.SemaphoreType.DMA((2,)),

time: 56.7 us -> 53.4 us (0.942)
  Pallas kernels: 54.7 us -> 51.4 us
    pallas_call x1, Pallas kernels: 54.7 us -> 51.4 us  [local(): pl.pallas_call(functools.partial(kernel, grid, slabs), out_shape=(pltpu.V...]
where the time goes in v3:
time: 53.4 us; the launch traced here: 53.3 us
  Pallas kernels  51.4 us (96%)
  local copies, waits for them, and re-layouts  1.25 us (2%)
  between operations  0.64 us (1%)
    pallas_call x1, Pallas kernels, local(): pl.pallas_call(functools.partial(kernel, grid, slabs), out_shape=(pltpu.V...  51.4 us
    unnamed x2, local copies, waits for them, and re-layouts  1.25 us

profile of v3, /device:TPU:1, one launch (start us, length us, event | category | flops | bytes accessed | tf_op | source)
XLA Modules:
  0.0 53.3 jit_solution(8514613569947610412)
XLA Ops:
  0.6 51.4 %two_gradients.1 = (bf16[8,2048]{1,0:T(8,128)(2,1)S(1)}, f32[128,128]{1,0:T(8,128)S(1)}) custom-call(f32[128,128]{1,0:T(8,128)} %bitcast.8, f32[8,32]{1,0:T(8,128)} %bitcast.11, s32[8]{0:T(128)} %frame_hbm.1, s32[8]{0:T(128)} %slot_hbm.1, bf16[4,128,256]{2,1,0:T(8,128)(2,1)} %w_hbm.1, s32[4,16,64]{2,1,0:T(8,128)} %bitcast.9, f32[3,4,8]{2,1,0:T(4,128)} %bitcast.10), custom_call_target="tpu_custom_call" | custom-call | tf_op jit(solution)/shard_map/two_gradients/pallas_call | solution.py:412
  52.1 0.6 %copy.12 = bf16[1,8,1,2048]{3,1,2,0:T(8,128)(2,1)} copy(bf16[1,8,1,2048]{3,1,2,0:T(8,128)(2,1)S(1)} %bitcast.7) | data formatting | bytes 65536
  52.7 0.6 %copy.13 = f32[8,1,2048]{2,1,0:T(1,128)} copy(f32[8,1,2048]{2,1,0:T(1,128)S(1)} %bitcast.6) | data formatting | bytes 131072

commit v4 on v3

--- a/solution.py
+++ b/solution.py
@@ -42,7 +42,7 @@
     meas_hbm, basis_hbm, frame_hbm, slot_hbm, w_hbm, off_hbm, cone_hbm,
     coef_ref, misfit_ref,
     meas_ref, basis_ref, frame_ref, slot_ref, w_ref, off_ref, cone_ref, load_sem,
-    meta_send, meta_recv, x_ref, ma_ref, mb_ref, near_ref, edge_ref, far_ref, plane_ref, planes_ref,
+    meta_send, meta_recv, x_ref, xt_ref, ma_ref, mb_ref, mta_ref, mtb_ref, near_ref, edge_ref, far_ref, plane_ref, planes_ref,
     r1_ref, r2_ref, p1_send, p1_recv, p2_send, p2_recv, first_ref, s_send, s_recv,
     g_ss, g_rs, c_ss, c_rs, z_ss, z_rs, h_ss, h_rs,
 ):
@@ -78,7 +78,7 @@
         (na, alpha, a_steps, a_at, a_device, lambda step: -step),
         (nb, beta, b_steps, b_at, b_device, lambda step: (-step[0], -step[1])),
     )
-    m_refs = (ma_ref, mb_ref)
+    m_refs, mt_refs = (ma_ref, mb_ref), (mta_ref, mtb_ref)
 
     def copy(kind, v, phase, n, src, dst):
         _, _, steps, _, device, _ = groups[(v + kind) % 2]
@@ -133,9 +133,6 @@
             (meas_hbm, meas_ref), (cone_hbm, cone_ref), (w_hbm, w_ref),
         ])
     ]
-    for load in loads:
-        load.start()
-
     sent = []
 
     def send(copy, valid=None):
@@ -153,14 +150,16 @@
                 pl.when(valid)(copy.wait_send)
 
     barrier = pltpu.get_barrier_semaphore()
+    for step in sorted(range(1, slabs), key=lambda d: -min(d, slabs - d)):
+        pl.semaphore_signal(
+            barrier, inc=1, device_id={"zslab": lax.rem(slab + step, slabs)}, device_id_type=MESH
+        )
     for step in a_steps:
         pl.semaphore_signal(barrier, inc=1, device_id={"angle": a_device(step)}, device_id_type=MESH)
     for step in b_steps:
         pl.semaphore_signal(barrier, inc=1, device_id={"angle": b_device(step)}, device_id_type=MESH)
-    for step in range(1, slabs):
-        pl.semaphore_signal(
-            barrier, inc=1, device_id={"zslab": lax.rem(slab + step, slabs)}, device_id_type=MESH
-        )
+    for load in loads:
+        load.start()
 
     for load in loads[:4]:
         load.wait()
@@ -188,11 +187,21 @@
     phi = lax.dot_general(
         basis_ref[...], hot, NN, precision=lax.Precision.HIGHEST, preferred_element_type=f32
     )
+    rows_p = iota((PROJ, 32), 0)
+    frames = jnp.zeros((PROJ, 32), i32)
+    for p in range(PROJ):
+        frames = jnp.where(rows_p == p, frame_ref[p], frames)
+    hot = (frames == iota((PROJ, 32), 1)).astype(f32)
+    phi_rows = lax.dot_general(
+        hot, jnp.concatenate([basis_ref[...]] * TILES, axis=0), NT,
+        precision=lax.Precision.HIGHEST, preferred_element_type=f32,
+    )
     for v in range(VIEWS):
         (ng, me, *_), (ns, *_) = groups[v], groups[1 - v]
         for g in range(ng):
             meta_send[v, g, 0:ns, :] = offs_sent[v][g * ns:(g + 1) * ns]
             meta_send[v, g, 8:16, :] = phi
+            meta_send[v, g, 16:24, :] = phi_rows
         meta_recv[v, me] = meta_send[v, me]
 
     for step in SLAB_OFFS:
@@ -268,6 +277,7 @@
 
     e_row, e_col = iota((TILE, TILE), 0), iota((TILE, TILE), 1)
     same = (e_row >> 4) == (e_col >> 4)
+    tile_row = iota((TILES, TILE), 0).astype(f32)
     tile_lane = (iota((BASIS, TILE), 1) & (TILES - 1)).astype(f32)
     for v in (1, 0):
         (ng, *_), (ns, *_), m_ref = groups[v], groups[1 - v], m_refs[v]
@@ -276,6 +286,9 @@
         for i in range(TILES):
             expand = jnp.logical_and(same, (e_row & (TILES - 1)) == i).astype(f32).astype(bf16)
             x_ref[v, i] = mm(near, expand)
+        for p in range(PROJ):
+            expand = jnp.logical_and(e_row >> 4 == p, (e_row & (TILES - 1)) == (e_col >> 3))
+            xt_ref[v, p] = mm(near, expand.astype(f32).astype(bf16))
         factors = [meta_recv[v, g, 8:16, :] for g in range(ng)]
 
         def build(b, carry):
@@ -288,6 +301,15 @@
                         lines.append(jnp.where(hit, factors[g], 0.0))
                     at = pl.ds(pl.multiple_of(b * TILE + pair * 16, 16), 16)
                     m_ref[at, g * TILE:(g + 1) * TILE] = jnp.concatenate(lines, axis=0).astype(bf16)
+            at = pl.ds(pl.multiple_of(b * TILE, TILE), TILE)
+            for g in range(ng):
+                for p in range(PROJ):
+                    line = xt_ref[v, p, pl.ds(g * ns + b, 1), :]
+                    hit = jnp.broadcast_to(line, (TILES, TILE)) == tile_row
+                    factor = jnp.broadcast_to(meta_recv[v, g, 16 + p:17 + p, :], (TILES, TILE))
+                    mt_refs[v][g * TILE + p * TILES:g * TILE + (p + 1) * TILES, at] = jnp.where(
+                        hit, factor, 0.0
+                    ).astype(bf16)
             return carry
 
         lax.fori_loop(0, ns, build, 0)
@@ -300,9 +322,9 @@
 
         def rows_of(v, pair):
             some = jnp.concatenate(
-                [m_refs[v][pl.ds(pl.multiple_of(b * TILE, TILE), TILE), :] for b in pair], axis=0
+                [mt_refs[v][:, pl.ds(pl.multiple_of(b * TILE, TILE), TILE)] for b in pair], axis=1
             )
-            value = mm(gathered[v], some, NT)
+            value = mm(gathered[v], some)
             return value[:, :TILE], value[:, TILE:]
 
         own = {}
@@ -358,17 +380,18 @@
                     continue
                 s_send[v, m] = value.astype(bf16)
                 send(copy(0, v, 2, m, s_send.at[v, m], s_recv.at[v, m]))
-    landed = jnp.zeros((TILE, 2 * TILE), f32)
     for v in (0, 1):
         wait_all(0, v, 2, lambda n, at: s_recv.at[v, n])
-        total = sums[v]
         for n in range(groups[v][0] - 1):
-            total = total + s_recv[v, n].astype(f32)
-        some = jnp.concatenate([w_ref[a, v * UC:(v + 1) * UC, :] for a in range(ANG)], axis=0)
-        owner = jnp.broadcast_to(slot_lane[:1], (UC, TILE))
-        masked = jnp.concatenate([jnp.where(owner == a, total, 0.0) for a in range(ANG)], axis=0)
-        for half in split(masked.T):
-            landed = landed + mm(half, some)
+            sums[v] = sums[v] + s_recv[v, n].astype(f32)
+    landed = jnp.zeros((TILE, 2 * TILE), f32)
+    for half in split(jnp.concatenate([sums[0], sums[1]], axis=0).T):
+        blank = jnp.zeros((TILES, TILE), bf16)
+        masked = jnp.concatenate([
+            jnp.concatenate([jnp.where(slots[p] == a, part(half, p), blank) for a in range(ANG)], axis=1)
+            for p in range(PROJ)
+        ], axis=0)
+        landed = landed + mm(masked, weights)
     plane = landed[:, :TILE] + shift_down(landed[:, TILE:])
     plane_ref[...] = plane.astype(bf16)
     for step in SLAB_OFFS:
@@ -426,11 +449,14 @@
             pltpu.VMEM((ANG, TILES, na * nb), i32),
             pltpu.SMEM((3, slabs, PROJ), f32),
             pltpu.SemaphoreType.DMA((7,)),
-            pltpu.VMEM((VIEWS, most, 16, TILE), f32),
-            pltpu.VMEM((VIEWS, most, 16, TILE), f32),
+            pltpu.VMEM((VIEWS, most, 24, TILE), f32),
+            pltpu.VMEM((VIEWS, most, 24, TILE), f32),
             pltpu.VMEM((VIEWS, TILES, na * nb, TILE), f32),
+            pltpu.VMEM((VIEWS, PROJ, na * nb, TILE), f32),
             pltpu.VMEM((nb * TILE, na * TILE), bf16),
             pltpu.VMEM((na * TILE, nb * TILE), bf16),
+            pltpu.VMEM((na * TILE, nb * TILE), bf16),
+            pltpu.VMEM((nb * TILE, na * TILE), bf16),
             pltpu.VMEM(block, f32),
             pltpu.VMEM(block, bf16),
             pltpu.VMEM(block, bf16),

time: 53.4 us -> 51.9 us (0.972)
  Pallas kernels: 51.4 us -> 49.9 us
    pallas_call x1, Pallas kernels: 51.4 us -> 49.9 us  [local(): pl.pallas_call(functools.partial(kernel, grid, slabs), out_shape=(pltpu.V...]
where the time goes in v4:
time: 51.9 us; the launch traced here: 51.8 us
  Pallas kernels  49.9 us (96%)
  local copies, waits for them, and re-layouts  1.25 us (2%)
  between operations  0.64 us (1%)
    pallas_call x1, Pallas kernels, local(): pl.pallas_call(functools.partial(kernel, grid, slabs), out_shape=(pltpu.V...  49.9 us
    unnamed x2, local copies, waits for them, and re-layouts  1.25 us

profile of v4, /device:TPU:1, one launch (start us, length us, event | category | flops | bytes accessed | tf_op | source)
XLA Modules:
  0.0 51.8 jit_solution(4018616644972722155)
XLA Ops:
  0.6 49.9 %two_gradients.1 = (bf16[8,2048]{1,0:T(8,128)(2,1)S(1)}, f32[128,128]{1,0:T(8,128)S(1)}) custom-call(f32[128,128]{1,0:T(8,128)} %bitcast.8, f32[8,32]{1,0:T(8,128)} %bitcast.11, s32[8]{0:T(128)} %frame_hbm.1, s32[8]{0:T(128)} %slot_hbm.1, bf16[4,128,256]{2,1,0:T(8,128)(2,1)} %w_hbm.1, s32[4,16,64]{2,1,0:T(8,128)} %bitcast.9, f32[3,4,8]{2,1,0:T(4,128)} %bitcast.10), custom_call_target="tpu_custom_call" | custom-call | tf_op jit(solution)/shard_map/two_gradients/pallas_call | solution.py:435
  50.5 0.6 %copy.12 = bf16[1,8,1,2048]{3,1,2,0:T(8,128)(2,1)} copy(bf16[1,8,1,2048]{3,1,2,0:T(8,128)(2,1)S(1)} %bitcast.7) | data formatting | bytes 65536
  51.2 0.6 %copy.13 = f32[8,1,2048]{2,1,0:T(1,128)} copy(f32[8,1,2048]{2,1,0:T(1,128)S(1)} %bitcast.6) | data formatting | bytes 131072

commit v5 on v4

--- a/solution.py
+++ b/solution.py
@@ -255,14 +255,14 @@
 
     def send_responses(phase, r_ref, back):
         high, low = split(jnp.concatenate([back, shift_up(back)], axis=1))
-        every = mm(weights, high, NT) + mm(weights, low, NT)
         owner = jnp.broadcast_to(slot_lane[:1], (UC, TILE))
         for v in range(VIEWS):
             ng, me, *_ = groups[v]
+            some = jnp.concatenate([w_ref[a, v * UC:(v + 1) * UC, :] for a in range(ANG)], axis=0)
+            every = mm(some, high, NT) + mm(some, low, NT)
             own = jnp.zeros((UC, TILE), f32)
             for a in range(ANG):
-                at = a * TILE + v * UC
-                own = jnp.where(owner == a, every[at:at + UC], own)
+                own = jnp.where(owner == a, every[a * UC:(a + 1) * UC], own)
             r_ref[v, me] = own.astype(bf16)
             for n in range(ng - 1):
                 send(copy(0, v, phase, n, r_ref.at[v, me], r_ref.at[v, me]))
@@ -340,19 +340,19 @@
                         continue
                     p_send[v, m] = value.astype(bf16)
                     send(copy(1, v, phase, m, p_send.at[v, m], p_recv.at[v, m]))
-        for v in (0, 1):
+        for v in (1, 0):
             wait_all(1, v, phase, lambda n, at: p_recv.at[v, n])
             total = own[v]
             for n in range(groups[1 - v][0] - 1):
                 total = total + p_recv[v, n].astype(f32)
             use(v, total)
 
-    firsts = []
+    firsts = {}
 
     def use_first(v, total):
         ns, me, *_ = groups[1 - v]
         first = (STEP * total).astype(bf16)
-        firsts.append(first.astype(f32))
+        firsts[v] = first.astype(f32)
         first_ref[v, me] = first
         for n in range(ns - 1):
             send(copy(1, v, 1, n, first_ref.at[v, me], first_ref.at[v, me]))
@@ -413,10 +413,10 @@
     misfit_ref[...] = misfit
 
     send_responses(3, r2_ref, back_of(misfit_at(-1), misfit, misfit_at(1)))
-    updates = []
-    scatter_gradient(2, 3, r2_ref, p2_send, p2_recv, lambda v, total: updates.append(total))
+    updates = {}
+    scatter_gradient(2, 3, r2_ref, p2_send, p2_recv, updates.__setitem__)
     rows_now = jnp.concatenate(
-        [first - STEP * update for first, update in zip(firsts, updates)], axis=0
+        [firsts[v] - STEP * updates[v] for v in range(VIEWS)], axis=0
     ).T.astype(bf16)
     coef_ref[...] = jnp.concatenate(
         [rows_now[i * BASIS:(i + 1) * BASIS] for i in range(TILES)], axis=1

time: 51.9 us -> 51.3 us (0.988)
  Pallas kernels: 49.9 us -> 49.3 us
    pallas_call x1, Pallas kernels: 49.9 us -> 49.3 us  [local(): pl.pallas_call(functools.partial(kernel, grid, slabs), out_shape=(pltpu.V...]
where the time goes in v5:
time: 51.3 us; the launch traced here: 51.2 us
  Pallas kernels  49.3 us (96%)
  local copies, waits for them, and re-layouts  1.25 us (2%)
  between operations  0.64 us (1%)
    pallas_call x1, Pallas kernels, local(): pl.pallas_call(functools.partial(kernel, grid, slabs), out_shape=(pltpu.V...  49.3 us
    unnamed x2, local copies, waits for them, and re-layouts  1.25 us

profile of v5, /device:TPU:1, one launch (start us, length us, event | category | flops | bytes accessed | tf_op | source)
XLA Modules:
  0.0 51.2 jit_solution(3111143490636002438)
XLA Ops:
  0.6 49.3 %two_gradients.1 = (bf16[8,2048]{1,0:T(8,128)(2,1)S(1)}, f32[128,128]{1,0:T(8,128)S(1)}) custom-call(f32[128,128]{1,0:T(8,128)} %bitcast.8, f32[8,32]{1,0:T(8,128)} %bitcast.11, s32[8]{0:T(128)} %frame_hbm.1, s32[8]{0:T(128)} %slot_hbm.1, bf16[4,128,256]{2,1,0:T(8,128)(2,1)} %w_hbm.1, s32[4,16,64]{2,1,0:T(8,128)} %bitcast.9, f32[3,4,8]{2,1,0:T(4,128)} %bitcast.10), custom_call_target="tpu_custom_call" | custom-call | tf_op jit(solution)/shard_map/two_gradients/pallas_call | solution.py:435
  50.0 0.6 %copy.12 = bf16[1,8,1,2048]{3,1,2,0:T(8,128)(2,1)} copy(bf16[1,8,1,2048]{3,1,2,0:T(8,128)(2,1)S(1)} %bitcast.7) | data formatting | bytes 65536
  50.6 0.6 %copy.13 = f32[8,1,2048]{2,1,0:T(1,128)} copy(f32[8,1,2048]{2,1,0:T(1,128)S(1)} %bitcast.6) | data formatting | bytes 131072

commit v6 on v5

--- a/solution.py
+++ b/solution.py
@@ -279,28 +279,19 @@
     same = (e_row >> 4) == (e_col >> 4)
     tile_row = iota((TILES, TILE), 0).astype(f32)
     tile_lane = (iota((BASIS, TILE), 1) & (TILES - 1)).astype(f32)
+    def near_of(v):
+        (ng, *_), (ns, *_) = groups[v], groups[1 - v]
+        near = jnp.concatenate([meta_recv[v, g, 0:ns, :] for g in range(ng)], axis=0).astype(bf16)
+        return ng, ns, near
+
     for v in (1, 0):
-        (ng, *_), (ns, *_), m_ref = groups[v], groups[1 - v], m_refs[v]
         wait_all(0, v, 0, lambda n, at: meta_recv.at[v, at])
-        near = jnp.concatenate([meta_recv[v, g, 0:ns, :] for g in range(ng)], axis=0).astype(bf16)
-        for i in range(TILES):
-            expand = jnp.logical_and(same, (e_row & (TILES - 1)) == i).astype(f32).astype(bf16)
-            x_ref[v, i] = mm(near, expand)
+        ng, ns, near = near_of(v)
         for p in range(PROJ):
             expand = jnp.logical_and(e_row >> 4 == p, (e_row & (TILES - 1)) == (e_col >> 3))
             xt_ref[v, p] = mm(near, expand.astype(f32).astype(bf16))
-        factors = [meta_recv[v, g, 8:16, :] for g in range(ng)]
-
-        def build(b, carry):
-            for pair in range(TILES // 2):
-                for g in range(ng):
-                    lines = []
-                    for i in (2 * pair, 2 * pair + 1):
-                        line = x_ref[v, i, pl.ds(g * ns + b, 1), :]
-                        hit = jnp.broadcast_to(line, (BASIS, TILE)) == tile_lane
-                        lines.append(jnp.where(hit, factors[g], 0.0))
-                    at = pl.ds(pl.multiple_of(b * TILE + pair * 16, 16), 16)
-                    m_ref[at, g * TILE:(g + 1) * TILE] = jnp.concatenate(lines, axis=0).astype(bf16)
+
+        def build_transposed(b, carry):
             at = pl.ds(pl.multiple_of(b * TILE, TILE), TILE)
             for g in range(ng):
                 for p in range(PROJ):
@@ -312,12 +303,36 @@
                     ).astype(bf16)
             return carry
 
-        lax.fori_loop(0, ns, build, 0)
+        lax.fori_loop(0, ns, build_transposed, 0)
+
+    def build_plain():
+        for v in (0, 1):
+            ng, ns, near = near_of(v)
+            for i in range(TILES):
+                expand = jnp.logical_and(same, (e_row & (TILES - 1)) == i).astype(f32).astype(bf16)
+                x_ref[v, i] = mm(near, expand)
+            factors = [meta_recv[v, g, 8:16, :] for g in range(ng)]
+
+            def build(b, carry):
+                for pair in range(TILES // 2):
+                    for g in range(ng):
+                        lines = []
+                        for i in (2 * pair, 2 * pair + 1):
+                            line = x_ref[v, i, pl.ds(g * ns + b, 1), :]
+                            hit = jnp.broadcast_to(line, (BASIS, TILE)) == tile_lane
+                            lines.append(jnp.where(hit, factors[g], 0.0))
+                        at = pl.ds(pl.multiple_of(b * TILE + pair * 16, 16), 16)
+                        m_refs[v][at, g * TILE:(g + 1) * TILE] = jnp.concatenate(
+                            lines, axis=0
+                        ).astype(bf16)
+                return carry
+
+            lax.fori_loop(0, ns, build, 0)
 
     def wide(ref, c, count):
         return jnp.concatenate([ref[c, j] for j in range(count)], axis=1)
 
-    def scatter_gradient(phase, g_phase, r_ref, p_send, p_recv, use):
+    def scatter_gradient(phase, g_phase, r_ref, p_send, p_recv, use, meanwhile=lambda: None):
         gathered = {}
 
         def rows_of(v, pair):
@@ -340,6 +355,7 @@
                         continue
                     p_send[v, m] = value.astype(bf16)
                     send(copy(1, v, phase, m, p_send.at[v, m], p_recv.at[v, m]))
+        meanwhile()
         for v in (1, 0):
             wait_all(1, v, phase, lambda n, at: p_recv.at[v, n])
             total = own[v]
@@ -357,7 +373,7 @@
         for n in range(ns - 1):
             send(copy(1, v, 1, n, first_ref.at[v, me], first_ref.at[v, me]))
 
-    scatter_gradient(0, 1, r1_ref, p1_send, p1_recv, use_first)
+    scatter_gradient(0, 1, r1_ref, p1_send, p1_recv, use_first, build_plain)
     fields = []
 
     def sums_of(v, pair):

time: 51.3 us -> 51 us (level)
  no operation moved by 1% of the time
where the time goes in v6:
time: 51 us; the launch traced here: 50.9 us
  Pallas kernels  49 us (96%)
  local copies, waits for them, and re-layouts  1.25 us (2%)
  between operations  0.64 us (1%)
    pallas_call x1, Pallas kernels, local(): pl.pallas_call(functools.partial(kernel, grid, slabs), out_shape=(pltpu.V...  49 us
    unnamed x2, local copies, waits for them, and re-layouts  1.25 us

profile of v6, /device:TPU:1, one launch (start us, length us, event | category | flops | bytes accessed | tf_op | source)
XLA Modules:
  0.0 50.9 jit_solution(14109359428885180608)
XLA Ops:
  0.6 49.0 %two_gradients.1 = (bf16[8,2048]{1,0:T(8,128)(2,1)S(1)}, f32[128,128]{1,0:T(8,128)S(1)}) custom-call(f32[128,128]{1,0:T(8,128)} %bitcast.8, f32[8,32]{1,0:T(8,128)} %bitcast.11, s32[8]{0:T(128)} %frame_hbm.1, s32[8]{0:T(128)} %slot_hbm.1, bf16[4,128,256]{2,1,0:T(8,128)(2,1)} %w_hbm.1, s32[4,16,64]{2,1,0:T(8,128)} %bitcast.9, f32[3,4,8]{2,1,0:T(4,128)} %bitcast.10), custom_call_target="tpu_custom_call" | custom-call | tf_op jit(solution)/shard_map/two_gradients/pallas_call | solution.py:451
  49.6 0.6 %copy.12 = bf16[1,8,1,2048]{3,1,2,0:T(8,128)(2,1)} copy(bf16[1,8,1,2048]{3,1,2,0:T(8,128)(2,1)S(1)} %bitcast.7) | data formatting | bytes 65536
  50.2 0.6 %copy.13 = f32[8,1,2048]{2,1,0:T(1,128)} copy(f32[8,1,2048]{2,1,0:T(1,128)S(1)} %bitcast.6) | data formatting | bytes 131072

commit v7 on v6

--- a/solution.py
+++ b/solution.py
@@ -400,14 +400,16 @@
         wait_all(0, v, 2, lambda n, at: s_recv.at[v, n])
         for n in range(groups[v][0] - 1):
             sums[v] = sums[v] + s_recv[v, n].astype(f32)
-    landed = jnp.zeros((TILE, 2 * TILE), f32)
-    for half in split(jnp.concatenate([sums[0], sums[1]], axis=0).T):
-        blank = jnp.zeros((TILES, TILE), bf16)
-        masked = jnp.concatenate([
-            jnp.concatenate([jnp.where(slots[p] == a, part(half, p), blank) for a in range(ANG)], axis=1)
-            for p in range(PROJ)
-        ], axis=0)
-        landed = landed + mm(masked, weights)
+    blank = jnp.zeros((TILES, TILE), bf16)
+    halves = split(jnp.concatenate([sums[0], sums[1]], axis=0).T)
+    masked = jnp.concatenate([
+        jnp.concatenate(
+            [jnp.where(slots[p] == a, part(half, p), blank) for half in halves for a in range(ANG)],
+            axis=1,
+        )
+        for p in range(PROJ)
+    ], axis=0)
+    landed = mm(masked, jnp.concatenate([weights, weights], axis=0))
     plane = landed[:, :TILE] + shift_down(landed[:, TILE:])
     plane_ref[...] = plane.astype(bf16)
     for step in SLAB_OFFS:

time: 51 us -> 50.9 us (level)
  no operation moved by 1% of the time
where the time goes in v7:
time: 50.9 us; the launch traced here: 50.8 us
  Pallas kernels  49 us (96%)
  local copies, waits for them, and re-layouts  1.25 us (2%)
  between operations  0.64 us (1%)
    pallas_call x1, Pallas kernels, local(): pl.pallas_call(functools.partial(kernel, grid, slabs), out_shape=(pltpu.V...  49 us
    unnamed x2, local copies, waits for them, and re-layouts  1.25 us

profile of v7, /device:TPU:1, one launch (start us, length us, event | category | flops | bytes accessed | tf_op | source)
XLA Modules:
  0.0 50.8 jit_solution(12912275818364575930)
XLA Ops:
  0.6 49.0 %two_gradients.1 = (bf16[8,2048]{1,0:T(8,128)(2,1)S(1)}, f32[128,128]{1,0:T(8,128)S(1)}) custom-call(f32[128,128]{1,0:T(8,128)} %bitcast.8, f32[8,32]{1,0:T(8,128)} %bitcast.11, s32[8]{0:T(128)} %frame_hbm.1, s32[8]{0:T(128)} %slot_hbm.1, bf16[4,128,256]{2,1,0:T(8,128)(2,1)} %w_hbm.1, s32[4,16,64]{2,1,0:T(8,128)} %bitcast.9, f32[3,4,8]{2,1,0:T(4,128)} %bitcast.10), custom_call_target="tpu_custom_call" | custom-call | tf_op jit(solution)/shard_map/two_gradients/pallas_call | solution.py:453
  49.6 0.6 %copy.12 = bf16[1,8,1,2048]{3,1,2,0:T(8,128)(2,1)} copy(bf16[1,8,1,2048]{3,1,2,0:T(8,128)(2,1)S(1)} %bitcast.7) | data formatting | bytes 65536
  50.2 0.6 %copy.13 = f32[8,1,2048]{2,1,0:T(1,128)} copy(f32[8,1,2048]{2,1,0:T(1,128)S(1)} %bitcast.6) | data formatting | bytes 131072
